TPU v7x, 256 devices: a whole 4x4x8 slice. The times are simulated.
256 devices in a mesh: sub: 2 (over core), row: 16 (over y, x), col: 8 (over z).
Axes of the slice: x: 4, y: 4, z: 8, core: 2. Of those that a mesh axis runs over, the one named last changes fastest.
Arguments:
- front_entries: float32 [4, 16, 128, 4, 16, 128], P(None, 'row', None, None, ('sub', 'col')), may hold values from -1 to 81, as said below
- child_updates: float32 [2, 3, 16, 128, 6, 8, 128], P('sub', None, 'row', None, None, 'col'), may hold values from -1 to 1, as said below
- row_maps: int32 [2, 48], replicated, may hold values from 0 to 63, as said below
Outputs:
- front_out: float32 [4, 16, 128, 4, 16, 128], P(None, 'row', None, None, ('sub', 'col'))
- factor: float32 [4, 16, 128, 1024], P(None, 'row')
Inputs may be any that keep to these rules, and one draw needn't show every extreme that they name: `row_maps`: each child's row is strictly increasing, begins at 0 and ends at 63. `front_entries`: Symmetric; in every draw the assembled front's leading 1024 x 1024 block is positive definite. `child_updates`: each child's update is symmetric.
All inputs are finite; a program needn't handle non-finite values.
Results may differ from a plain program's by a relative error of at most 0.00016.
Values sent between devices are 32-bit elements; how exact they have to be, the bound alone decides.
No kernel may reach another device: no remote copies, remote signals or barrier semaphores. Data moves between devices by JAX's collectives and lax.ppermute only.
A program may use at most 128 MiB of HBM per device.

v0:
```python
import functools

import jax
import jax.numpy as jnp
from jax import lax
from jax.experimental import pallas as pl
from jax.experimental.pallas import tpu as pltpu
from jax.sharding import PartitionSpec as P

BLK = 128
FB = 64
UB = 48
P_SIZE = 1024
NPB = 8
GR = 16
NC = 8
CHIPS = GR * NC
F32 = jnp.float32
HIGHEST = lax.Precision.HIGHEST


def dot_full(a, b, dim_a, dim_b):
    return lax.dot_general(
        a, b, (((dim_a,), (dim_b,)), ((), ())), precision=HIGHEST, preferred_element_type=F32
    )


def split(x):
    high = x.astype(jnp.bfloat16)
    return high, (x - high.astype(F32)).astype(jnp.bfloat16)


def dot_split(a, b):
    left = jnp.concatenate([a[0], a[0], a[1]], 1)
    right = jnp.concatenate([b[0], b[1], b[0]], 1)
    return lax.dot_general(left, right, (((1,), (1,)), ((), ())), preferred_element_type=F32)


def split_rows(x):
    def head(y):
        return y.astype(jnp.bfloat16).astype(F32)

    high = head(x)
    mid = head(x - high)
    return high, mid, head(x - high - mid)


def stacked(parts):
    return jnp.concatenate(parts, 0).astype(jnp.bfloat16)


def reciprocal(x):
    guess = pltpu.reciprocal(x, approx=True)
    return guess * (2.0 - x * guess)


def row_of(x, t):
    return jnp.broadcast_to(x[t : t + 1, :], x.shape)


def col_of(x, t):
    return jnp.broadcast_to(x[:, t : t + 1], x.shape)


def products(columns, rows):
    parts = [c * r for c, r in zip(columns, rows, strict=True)]
    while len(parts) > 1:
        parts = [parts[2 * n] + parts[2 * n + 1] for n in range(len(parts) // 2)]
    return parts[0]


NEAR = 2


def factor_block(w):
    sub = lax.broadcasted_iota(jnp.int32, (8, BLK), 0)
    lane = lax.broadcasted_iota(jnp.int32, (8, BLK), 1)
    tiles = BLK // 8
    left = [w[8 * i : 8 * i + 8, :] for i in range(tiles)]
    right = [(lane == sub + 8 * i).astype(F32) for i in range(tiles)]
    uppers, inverses = [], []
    diag = [col_of(left[0], t) for t in range(8)]
    for s in range(tiles):
        rows, extra = left[s], right[s]
        raw, last = rows, s == tiles - 1
        ahead, later, near = [], [], {}
        if not last:
            ahead = [col_of(rows, 8 * s + 8 + t) for t in range(8)]
            later = [col_of(left[s + 1], 8 * s + 8 + t) for t in range(8)]
            near = {
                i: [col_of(left[i], 8 * s + t) for t in range(8)]
                for i in range(s + 1, min(tiles, s + 1 + NEAR))
            }
        u, v, pivots = rows, extra, None
        for t in range(0, 8, 2):
            c0, c1 = diag[t], diag[t + 1]
            a, b, d = row_of(c0, t), row_of(c1, t), row_of(c1, t + 1)
            inv_det = reciprocal(a * d - b * b)
            at0, at1 = sub == t, sub == t + 1
            either = at0 | at1
            g0 = jnp.where(at0, -d, jnp.where(at1, b, c0 * d - c1 * b))
            g1 = jnp.where(at0, b, jnp.where(at1, -a, c1 * a - c0 * b))
            h0, h1 = g0 * inv_det, g1 * inv_det
            ratio = b * reciprocal(a)
            u = jnp.where(at0, rows, jnp.where(at1, row_of(rows, t + 1) - ratio * row_of(rows, t), u))
            v = jnp.where(
                at0, extra, jnp.where(at1, row_of(extra, t + 1) - ratio * row_of(extra, t), v)
            )
            pivots = a if pivots is None else jnp.where(at0, a, pivots)
            pivots = jnp.where(at1, d - b * ratio, pivots)

            def reduce(x, soon=False):
                x0, x1, base = row_of(x, t), row_of(x, t + 1), jnp.where(either, 0.0, x)
                if soon:
                    return base - (g0 * x0 + g1 * x1) * inv_det
                return base - (h0 * x0 + h1 * x1)

            for c in range(t + 2, 8):
                diag[c] = reduce(diag[c], c < t + 4)
            ahead = [reduce(x) for x in ahead]
            rows, extra = reduce(rows), reduce(extra)
        scale = lax.rsqrt(pivots)
        uppers.append(jnp.where(lane >= sub + 8 * s, u * scale, 0.0))
        inverses.append(v * scale)
        if last:
            break
        diag = [
            later[c] - products(near[s + 1], [row_of(ahead[c], t) for t in range(8)])
            for c in range(8)
        ]
        row_terms = [row_of(rows, t) for t in range(8)]
        extra_terms = [row_of(extra, t) for t in range(8)]
        for i, columns in near.items():
            left[i] = left[i] - products(columns, row_terms)
            right[i] = right[i] - products(columns, extra_terms)
        if s + 1 + NEAR < tiles:
            high, mid, low = split_rows(raw)
            far_columns = stacked([high, high, mid, mid, high, low])
            high, mid, low = split_rows(jnp.concatenate([rows, extra], 1))
            far_rows = stacked([high, mid, high, mid, low, high])
            far = lax.dot_general(
                far_columns, far_rows, (((0,), (0,)), ((), ())), preferred_element_type=F32
            )
            for i in range(s + 1 + NEAR, tiles):
                left[i] = left[i] - far[8 * i : 8 * i + 8, :BLK]
                right[i] = right[i] - far[8 * i : 8 * i + 8, BLK:]
    return jnp.concatenate(uppers, 0), jnp.concatenate(inverses, 0)


WIDE = 2 * BLK
CHUNK = 512
STRIP = 4 * BLK
STEPS = P_SIZE // WIDE
TRIANGLE = [(p, q) for q in range(NPB) for p in range(q, NPB)]
HALF = len(TRIANGLE) // 2


def cholesky_kernel(
    where_ref,
    own_ref,
    other_ref,
    low_hi,
    low_lo,
    inv_hi,
    inv_lo,
    top_ref,
    lower_ref,
    inverse_ref,
    panel,
    upper,
):
    first_core, grid_row = where_ref[0] == 0, where_ref[1]
    lower_ref[...] = jnp.zeros_like(lower_ref)

    def step(k, carry):
        for n in range(NPB):

            @pl.when(k == n)
            def _(n=n):
                start = n * BLK
                cols = slice(start, start + BLK)
                for p in range(n, NPB):
                    spot = TRIANGLE.index((p, n))
                    rows = slice(spot % HALF * 8, spot % HALF * 8 + 8)
                    own = own_ref[:, rows, :].reshape(BLK, BLK)
                    other = other_ref[:, rows, :].reshape(BLK, BLK)
                    is_own = first_core if spot < HALF else jnp.logical_not(first_core)
                    panel[(p - n) * BLK : (p - n + 1) * BLK, :] = jnp.where(is_own, own, other)
                if n:
                    panel[: P_SIZE - start, :] -= dot_full(
                        lower_ref[start:, :start], lower_ref[cols, :start], 1, 1
                    )

        u, v = factor_block(panel[:BLK, :])
        upper[...] = u
        inverse_ref[k] = v
        for n in range(NPB):

            @pl.when(k == n)
            def _(n=n):
                start = n * BLK
                cols = slice(start, start + BLK)
                lower_ref[cols, cols] = upper[...].T
                if n < NPB - 1:
                    lower_ref[start + BLK :, cols] = dot_full(
                        panel[BLK : P_SIZE - start, :], inverse_ref[n], 1, 1
                    )

        return carry

    lax.fori_loop(0, NPB, step, 0)
    top_ref[...] = lower_ref[
        pl.ds(pl.multiple_of(jnp.minimum(grid_row, NPB - 1) * BLK, BLK), BLK), :
    ]
    low_hi[...], low_lo[...] = split(lower_ref[...])
    for n in range(STEPS):
        a, b = inverse_ref[2 * n], inverse_ref[2 * n + 1]
        mid = lower_ref[(2 * n + 1) * BLK : (2 * n + 2) * BLK, 2 * n * BLK : (2 * n + 1) * BLK]
        corner = -dot_full(dot_full(b, mid, 1, 0), a, 1, 0)
        whole = jnp.concatenate(
            [
                jnp.concatenate([a, jnp.zeros((BLK, BLK), F32)], 1),
                jnp.concatenate([corner, b], 1),
            ],
            0,
        )
        inv_hi[n], inv_lo[n] = split(whole)


def cholesky(where, own, other):
    bf16 = jnp.bfloat16
    whole = pl.BlockSpec(memory_space=pltpu.VMEM)
    return pl.pallas_call(
        cholesky_kernel,
        in_specs=[pl.BlockSpec(memory_space=pltpu.SMEM), whole, whole],
        out_specs=[whole] * 5,
        out_shape=[jax.ShapeDtypeStruct((P_SIZE, P_SIZE), bf16)] * 2
        + [jax.ShapeDtypeStruct((STEPS, WIDE, WIDE), bf16)] * 2
        + [jax.ShapeDtypeStruct((BLK, P_SIZE), F32)],
        scratch_shapes=[
            pltpu.VMEM((P_SIZE, P_SIZE), F32),
            pltpu.VMEM((NPB, BLK, BLK), F32),
            pltpu.VMEM((P_SIZE, BLK), F32),
            pltpu.VMEM((BLK, BLK), F32),
        ],
        compiler_params=pltpu.CompilerParams(vmem_limit_bytes=60 * 2**20),
        cost_estimate=pl.CostEstimate(
            flops=1, bytes_accessed=1, transcendentals=0
        ),
        name="cholesky",
    )(where, own, other)


def solve_strip(strip, lower, inverse, keep):
    for m in range(STRIP // CHUNK):
        rows = slice(m * CHUNK, (m + 1) * CHUNK)
        high, low = [], []
        for n in range(STEPS):
            cols = slice(n * WIDE, (n + 1) * WIDE)
            part = strip[rows, cols]
            if n:
                done = slice(0, n * WIDE)
                part = part - dot_split(
                    (jnp.concatenate(high, 1), jnp.concatenate(low, 1)),
                    (lower[0][cols, done], lower[1][cols, done]),
                )
            part = dot_split(split(part), (inverse[0][n], inverse[1][n]))
            hi, lo = split(part)
            high.append(hi)
            low.append(lo)
            keep(rows, cols, part, hi, lo)


def column_kernel(
    col_hbm,
    low_hi_hbm,
    low_lo_hbm,
    inv_hi_hbm,
    inv_lo_hbm,
    col_hi,
    col_lo,
    col_ref,
    low_hi,
    low_lo,
    inv_hi,
    inv_lo,
    strip,
    sems,
):
    pairs = [
        (col_hbm, col_ref),
        (inv_hi_hbm, inv_hi),
        (inv_lo_hbm, inv_lo),
        (low_hi_hbm, low_hi),
        (low_lo_hbm, low_lo),
    ]
    loads = [pltpu.make_async_copy(a, b, sems.at[n]) for n, (a, b) in enumerate(pairs)]
    for load in loads:
        load.start()
    loads[0].wait()
    for b in range(4):
        part = jnp.swapaxes(col_ref[:, b * NPB : (b + 1) * NPB, :], 0, 1)
        for q in range(NPB):
            cols = slice(q * BLK, (q + 1) * BLK)
            strip[b * BLK : (b + 1) * BLK, cols] = part[q]
    for load in loads[1:]:
        load.wait()

    def keep(rows, cols, x, hi, lo):
        col_hi[rows, cols], col_lo[rows, cols] = hi, lo

    solve_strip(strip, (low_hi, low_lo), (inv_hi, inv_lo), keep)


def solve_columns(col_strip, *factor_parts):
    inputs = (col_strip, *factor_parts)
    anywhere = pl.BlockSpec(memory_space=pl.ANY)
    return pl.pallas_call(
        column_kernel,
        in_specs=[anywhere] * len(inputs),
        out_specs=[pl.BlockSpec(memory_space=pltpu.VMEM)] * 2,
        out_shape=[jax.ShapeDtypeStruct((STRIP, P_SIZE), jnp.bfloat16)] * 2,
        scratch_shapes=[pltpu.VMEM(x.shape, x.dtype) for x in inputs]
        + [pltpu.VMEM((STRIP, P_SIZE), F32), pltpu.SemaphoreType.DMA((len(inputs),))],
        compiler_params=pltpu.CompilerParams(vmem_limit_bytes=60 * 2**20),
        cost_estimate=pl.CostEstimate(
            flops=200_000_000_000, bytes_accessed=9_000_000, transcendentals=0
        ),
        name="solve_columns",
    )(*inputs)


def solve_kernel(
    where_ref,
    top_hbm,
    own_hbm,
    other_hbm,
    entry_hbm,
    col_hi_hbm,
    col_lo_hbm,
    low_hi_hbm,
    low_lo_hbm,
    inv_hi_hbm,
    inv_lo_hbm,
    factor_hbm,
    out_hbm,
    top_ref,
    own_ref,
    other_ref,
    entry_ref,
    col_hi,
    col_lo,
    low_hi,
    low_lo,
    inv_hi,
    inv_lo,
    factor_ref,
    out_ref,
    strip,
    row_hi,
    row_lo,
    sems,
):
    first_core, grid_row, grid_col = where_ref[0] == 0, where_ref[1], where_ref[2]
    pairs = [
        (own_hbm, own_ref),
        (other_hbm, other_ref),
        (inv_hi_hbm, inv_hi),
        (inv_lo_hbm, inv_lo),
        (low_hi_hbm, low_hi),
        (low_lo_hbm, low_lo),
        (col_hi_hbm, col_hi),
        (col_lo_hbm, col_lo),
        (top_hbm, top_ref),
        (entry_hbm, entry_ref),
    ]
    loads = [pltpu.make_async_copy(a, b, sems.at[n]) for n, (a, b) in enumerate(pairs)]
    for load in loads:
        load.start()
    for load in loads[:2]:
        load.wait()
    for b in range(4):
        is_own = first_core if b < 2 else jnp.logical_not(first_core)
        half = b % 2 * NPB
        own, other = own_ref[:, 16 + half : 24 + half, :], other_ref[:, half : half + NPB, :]
        picked = jnp.swapaxes(jnp.where(is_own, own, other), 0, 1)
        for q in range(NPB):
            strip[b * BLK : (b + 1) * BLK, q * BLK : (q + 1) * BLK] = picked[q]
    for load in loads[2:6]:
        load.wait()

    def keep_row(rows, cols, x, hi, lo):
        factor_ref[rows, cols] = x
        row_hi[rows, cols], row_lo[rows, cols] = hi, lo

    solve_strip(strip, (low_hi, low_lo), (inv_hi, inv_lo), keep_row)
    for load in loads[6:]:
        load.wait()

    @pl.when(grid_row < NPB)
    def _():
        factor_ref[:BLK, :] = top_ref[...]

    factor_store = pltpu.make_async_copy(factor_ref, factor_hbm, sems.at[10])
    factor_store.start()
    for b in range(4):
        rows = slice(b * BLK, (b + 1) * BLK)
        strip[rows, :STRIP] = dot_split(
            (row_hi[rows, :], row_lo[rows, :]), (col_hi[...], col_lo[...])
        )
        if b % 2 == 0:
            all_sums = jnp.swapaxes(own_ref[:, b * 4 : b * 4 + 8, :], 0, 1)
        for d in range(4):
            sums = all_sums[b % 2 * 4 + d]
            if b < d:
                sums = sums.T
            elif b == d:
                sums = jnp.where(grid_row >= grid_col, sums, sums.T)
            spot = pl.ds(b * STRIP + d, BLK, stride=4)
            block = entry_ref[spot, :] + sums
            trail = strip[rows, d * BLK : (d + 1) * BLK]
            if b == 0:
                trail = jnp.where(grid_row >= NPB, trail, 0.0)
            if d == 0:
                trail = jnp.where(grid_col >= NPB, trail, 0.0)
            out_ref[spot, :] = block - trail
    out_store = pltpu.make_async_copy(out_ref, out_hbm, sems.at[11])
    out_store.start()
    factor_store.wait()
    out_store.wait()


def solve_and_update(where, top, own, other, entries, *solved):
    bf16 = jnp.bfloat16
    inputs = (top, own, other, entries, *solved)
    outputs = [
        jax.ShapeDtypeStruct((STRIP, P_SIZE), F32),
        jax.ShapeDtypeStruct((4 * STRIP, BLK), F32),
    ]
    anywhere = pl.BlockSpec(memory_space=pl.ANY)
    return pl.pallas_call(
        solve_kernel,
        in_specs=[pl.BlockSpec(memory_space=pltpu.SMEM)] + [anywhere] * len(inputs),
        out_specs=[anywhere] * 2,
        out_shape=outputs,
        scratch_shapes=[pltpu.VMEM(x.shape, x.dtype) for x in (*inputs, *outputs)]
        + [pltpu.VMEM((STRIP, P_SIZE), F32)]
        + [pltpu.VMEM((STRIP, P_SIZE), bf16)] * 2
        + [pltpu.SemaphoreType.DMA((12,))],
        compiler_params=pltpu.CompilerParams(vmem_limit_bytes=60 * 2**20),
        cost_estimate=pl.CostEstimate(
            flops=6_000_000_000, bytes_accessed=14_000_000, transcendentals=0
        ),
        name="solve_and_update",
    )(where, *inputs)


def pack_kernel(inverse_map_ref, own_ref, other_ref, panel_ref, out_ref):
    for p in range(FB):
        b, r = divmod(p, GR)
        total = jnp.zeros((4 * NC, BLK), F32)
        for k, child in enumerate((own_ref, other_ref)):
            spot = inverse_map_ref[k, p]
            total = total + jnp.where(spot >= 0, child[jnp.maximum(spot, 0)], 0.0)
        for d in range(4):
            out_ref[pl.ds(r * 256 + b * 4 + d, NC, stride=32), :] = total[d * NC : (d + 1) * NC]
    for h in range(2):
        for r in range(GR):
            rows = panel_ref[h, r]
            for c in range(NC):
                out_ref[pl.ds(r * 256 + c * 32 + 16 + h * 8, NPB), :] = rows


def pack(inverse_maps, own, other, panel):
    whole = pl.BlockSpec(memory_space=pltpu.VMEM)
    return pl.pallas_call(
        pack_kernel,
        in_specs=[pl.BlockSpec(memory_space=pltpu.SMEM)] + [whole] * 3,
        out_specs=whole,
        out_shape=jax.ShapeDtypeStruct((CHIPS * 32, BLK), F32),
        compiler_params=pltpu.CompilerParams(vmem_limit_bytes=12 * 2**20),
        cost_estimate=pl.CostEstimate(flops=0, bytes_accessed=8_000_000, transcendentals=0),
        name="pack",
    )(inverse_maps, own, other, panel)


def to_chips(x):
    return lax.all_to_all(x, ("row", "col"), 0, 0)


def after(x, earlier):
    return lax.optimization_barrier((x, earlier))[0]


def swap_cores(x):
    return lax.ppermute(x, "sub", [(0, 1), (1, 0)])


def per_device(front_entries, child_updates, row_maps):
    my_row = lax.axis_index("row")
    my_col = lax.axis_index("col")
    my_sub = lax.axis_index("sub")
    entries = front_entries[:, 0, :, :, 0, :]
    child_own = child_updates[0, :, 0, :, :, 0, :]
    own_map = lax.dynamic_index_in_dim(row_maps, my_sub, 0, keepdims=False)
    other_map = lax.dynamic_index_in_dim(row_maps, 1 - my_sub, 0, keepdims=False)
    blocks = jnp.arange(FB, dtype=jnp.int32)
    where = jnp.stack([my_sub, my_row, my_sub * NC + my_col]).astype(jnp.int32)

    entry_panel = entries[:, :, 0, :]
    from_first = swap_cores(entry_panel[2:])
    entry_half = jnp.where(my_sub == 0, entry_panel[:2], from_first)
    counts = [2 * b + 2 for b in range(3)]
    slices_out = jnp.concatenate(
        [child_own[b, :, :count, :] for b, count in enumerate(counts)]
        + [entry_half.transpose(1, 0, 2)],
        1,
    )
    slices_in = to_chips(slices_out).reshape(GR, NC, 14, BLK)
    lower_child, start = [], 0
    for count in counts:
        part = slices_in[:, :, start : start + count].transpose(0, 2, 1, 3)
        part = jnp.pad(part, ((0, 0), (0, 6 - count), (0, 0), (0, 0)))
        lower_child.append(part.reshape(GR, UB, BLK))
        start += count
    lower_child = jnp.concatenate(lower_child, 0)
    entry_rows = slices_in[:, :, start:].transpose(2, 0, 1, 3).reshape(FB // 2, NPB, BLK)

    row_pick = (own_map[None, :] == blocks[:, None]).astype(F32)
    col_pick = (own_map[None, :NPB] == blocks[:NPB, None]).astype(F32)
    both_pick = (row_pick[:, None, :, None] * col_pick[None, :, None, :]).reshape(
        FB * NPB, UB * NPB
    )
    child_panel = lower_child[:, :NPB].reshape(UB * NPB, BLK)
    placed = dot_full(both_pick, child_panel, 1, 0).reshape(FB, NPB, BLK)
    no_rows = jnp.zeros_like(entry_rows)
    placed = placed + jnp.concatenate(
        [
            jnp.where(my_sub == 0, entry_rows, no_rows),
            jnp.where(my_sub == 0, no_rows, entry_rows),
        ],
        0,
    )
    panel_rows = placed + swap_cores(placed)

    by_grid = panel_rows.reshape(4, 2, NC, NPB, BLK)
    for_cols = lax.dynamic_index_in_dim(by_grid, my_sub, 1, keepdims=False).transpose(1, 0, 2, 3)
    triangle = jnp.concatenate([panel_rows[q:NPB, q] for q in range(NPB)], 0)
    triangle = lax.dynamic_index_in_dim(triangle.reshape(2, HALF, BLK), my_sub, 0, False)
    triangle = jnp.broadcast_to(triangle[None], (NC, HALF, BLK))
    along_col = lax.all_to_all(
        jnp.concatenate([for_cols.reshape(NC, 32, BLK), triangle], 1), "col", 0, 0
    )
    col_part = along_col[:, :32]
    col_strip = lax.all_gather(col_part, "row", axis=0)
    lead = along_col[:, 32:].transpose(1, 0, 2).reshape(HALF * 8, BLK)
    lead = after(lead, col_part)
    lead = lax.all_to_all(jnp.broadcast_to(lead[None], (GR, HALF * 8, BLK)), "row", 0, 0)

    ids = jnp.arange(UB, dtype=jnp.int32)
    below = (ids[:, None] > ids[None, :])[:, :, None]
    on_or_below = (ids[:, None] >= ids[None, :])[:, :, None]
    lower_child = after(lower_child, along_col)
    child = jnp.where(on_or_below, lower_child, 0.0)
    child = child + jnp.where(below, lower_child, 0.0).transpose(1, 0, 2)
    col_ids = blocks.reshape(4, 2, NC)
    own_cols = lax.dynamic_index_in_dim(col_ids, my_sub, 1, keepdims=False).reshape(-1)
    other_cols = lax.dynamic_index_in_dim(col_ids, 1 - my_sub, 1, keepdims=False).reshape(-1)
    all_cols = jnp.concatenate([own_cols, other_cols])
    widen = (own_map[None, :] == all_cols[:, None]).astype(F32)
    widened = jnp.einsum("qj,ijl->iql", widen, child, precision=HIGHEST)
    kept, arrived = widened[:, : FB // 2], swap_cores(widened[:, FB // 2 :])

    both_maps = jnp.stack([own_map, other_map])
    hit = both_maps[:, None, :] == blocks[None, :, None]
    inverse_maps = jnp.max(jnp.where(hit, ids, -1), axis=2)
    halves = panel_rows.reshape(2, 2, GR, NPB, BLK)
    for_rows = lax.dynamic_index_in_dim(halves, my_sub, 0, keepdims=False)
    rows_out = pack(inverse_maps, kept, arrived, for_rows).reshape(CHIPS, 32, BLK)
    lead, rows_out = lax.optimization_barrier((lead, rows_out))
    other_lead = swap_cores(lead)
    rows_in = to_chips(after(rows_out, other_lead))

    *factor_parts, top = cholesky(where, lead, other_lead)
    columns = solve_columns(col_strip.reshape(CHIPS, 32, BLK), *factor_parts)
    rows_in = after(rows_in, columns[0])
    factor, updated = solve_and_update(
        where,
        top,
        rows_in,
        swap_cores(rows_in[:, 16:]),
        entries.reshape(4 * STRIP, BLK),
        *columns,
        *factor_parts,
    )
    updated = updated.reshape(4, 1, BLK, 4, 1, BLK)
    return updated, factor.reshape(4, 1, BLK, P_SIZE)


def solution(mesh):
    in_specs = (
        P(None, "row", None, None, ("sub", "col"), None),
        P("sub", None, "row", None, None, "col", None),
        P(),
    )
    out_specs = (P(None, "row", None, None, ("sub", "col"), None), P(None, "row", None, None))
    return jax.shard_map(
        per_device, mesh=mesh, in_specs=in_specs, out_specs=out_specs, check_vma=False
    )
```

profile of v0, /device:TPU:1, one launch (start us, length us, event | category | flops | bytes accessed | tf_op | source)
XLA Modules:
  0.0 199.2 jit_solution(15257449325336057670)
XLA Ops:
  7.2 1.4 copy.119
  9.3 3.2 %collective-permute-start = (f32[2,128,128]{2,1,0:T(8,128)}, f32[2,128,128]{2,1,0:T(8,128)S(1)}, u32[]{:S(2)}, u32[]{:S(2)}) collective-permute-start(f32[2,128,128]{2,1,0:T(8,128)} %slice_bitcast_fusion.4), channel_id=1, source_target_pairs={{0,128},{128,0},{1,129},{129,1},{2,130},{130,2},{3,131},{131,3},{4... | collective-permute-start | bytes 393224 | tf_op jit(solution)/shard_map/ppermute | solution.py:496
  13.8 1.5 copy.78
  15.3 13.9 %all-to-all-start = ((f32[128,14,128]{2,1,0:T(8,128)}), f32[128,14,128]{2,1,0:T(8,128)S(1)}, u32[]{:S(2)}, u32[]{:S(2)}) async-start(f32[128,14,128]{2,1,0:T(8,128)} %copy.78), calls=%async_computation | async-start | bytes 2097152 | tf_op jit(solution)/shard_map/all_to_all | solution.py:488
  29.6 30.4 %all-to-all-done = f32[128,14,128]{2,1,0:T(8,128)S(1)} async-done(((f32[128,14,128]{2,1,0:T(8,128)}), f32[128,14,128]{2,1,0:T(8,128)S(1)}, u32[]{:S(2)}, u32[]{:S(2)}) %all-to-all-start) | async-done | bytes 917536 | tf_op jit(solution)/shard_map/all_to_all | solution.py:488
  60.8 1.9 fusion.6
  62.7 2.2 %collective-permute-start.1 = (f32[64,8,128]{2,1,0:T(8,128)S(1)}, f32[64,8,128]{2,1,0:T(8,128)S(1)}, u32[]{:S(2)}, u32[]{:S(2)}) collective-permute-start(f32[64,8,128]{2,1,0:T(8,128)S(1)} %fusion.6), channel_id=1, source_target_pairs={{0,128},{128,0},{1,129},{129,1},{2,130},{130,2},{3,131},{131,3},{4... | collective-permute-start | bytes 786440 | tf_op jit(solution)/shard_map/ppermute | solution.py:496
  65.0 1.2 collective-permute-done.1
  66.7 14.0 %all_to_all.20 = f32[8,50,128]{2,1,0:T(8,128)S(1)} all-to-all(f32[8,50,128]{2,1,0:T(8,128)S(1)} %pad_maximum_fusion.2), channel_id=1, replica_groups=mesh['sub'=2,'row'=16,'col'=8] {'col'}, dimensions={0} | all-to-all | bytes 409600 | tf_op jit(solution)/shard_map/all_to_all | solution.py:551
  82.8 3.7 %all-to-all-start.2 = ((f32[16,144,128]{2,1,0:T(8,128)}), f32[16,144,128]{2,1,0:T(8,128)S(1)}, u32[]{:S(2)}, u32[]{:S(2)}) async-start(f32[16,144,128]{2,1,0:T(8,128)} %broadcast_in_dim.62), calls=%async_computation.2 | async-start | bytes 2359296 | tf_op jit(solution)/shard_map/all_to_all | solution.py:558
  86.5 1.5 convolution_bitcast_fusion
  88.9 1.8 collective-permute-done.2.other_ref
  90.7 2.8 %pack.1 = f32[4096,128]{1,0:T(8,128)} custom-call(s32[2,64]{1,0:T(2,128)S(1)} %select_reduce_fusion.inverse_map_ref, f32[48,32,128]{2,1,0:T(8,128)S(1)} %get-tuple-element.45.own_ref, f32[48,32,128]{2,1,0:T(8,128)S(1)} %collective-permute-done.2.other_ref, f32[2,16,8,128]{3,2,1,0:T(8,128)S(1)} %dynamic-slice_bitcast_fusion.panel_ref), custom_call_target="tpu_custom_call" | custom-call | bytes 8000000 | tf_op jit(solution)/shard_map/pack/pallas_call | solution.py:476
  93.5 12.6 %all-to-all-done.2.own_ref = f32[16,144,128]{2,1,0:T(8,128)S(1)} async-done(((f32[16,144,128]{2,1,0:T(8,128)}), f32[16,144,128]{2,1,0:T(8,128)S(1)}, u32[]{:S(2)}, u32[]{:S(2)}) %all-to-all-start.2) | async-done | bytes 1179680 | tf_op jit(solution)/shard_map/all_to_all | solution.py:558
  106.1 2.0 %collective-permute-start.3 = (f32[16,144,128]{2,1,0:T(8,128)S(1)}, f32[16,144,128]{2,1,0:T(8,128)S(1)}, u32[]{:S(2)}, u32[]{:S(2)}) collective-permute-start(f32[16,144,128]{2,1,0:T(8,128)S(1)} %all-to-all-done.2.own_ref), channel_id=1, source_target_pairs={{0,128},{128,0},{1,129},{129,1},{2,130},{130,2},{3,131},{131,3},{4... | collective-permute-start | bytes 3538952 | tf_op jit(solution)/shard_map/ppermute | solution.py:496
  108.7 1.9 collective-permute-done.3.other_ref
  111.7 7.5 %all-to-all-start.3 = ((f32[128,32,128]{2,1,0:T(8,128)}), f32[128,32,128]{2,1,0:T(8,128)}, u32[]{:S(2)}, u32[]{:S(2)}) async-start(f32[128,32,128]{2,1,0:T(8,128)} %bitcast.43), calls=%async_computation.3 | async-start | bytes 4194304 | tf_op jit(solution)/shard_map/all_to_all | solution.py:488
  119.2 39.3 %cholesky.1 = (bf16[1024,1024]{1,0:T(8,128)(2,1)}, bf16[1024,1024]{1,0:T(8,128)(2,1)}, bf16[4,256,256]{2,1,0:T(8,128)(2,1)}, bf16[4,256,256]{2,1,0:T(8,128)(2,1)}, f32[128,1024]{1,0:T(8,128)}) custom-call(s32[3]{0:T(128)} %pad_add_fusion.1.where_ref, f32[16,144,128]{2,1,0:T(8,128)} %copy-done, f32[16,144,128]{2,1,0:T(8,128)} %copy-done.1), custom_call_target="tpu_custom_call" | custom-call | flops 1 | bytes 1 | tf_op jit(solution)/shard_map/cholesky/pallas_call | solution.py:233
  158.4 8.7 %solve_columns.1 = (bf16[512,1024]{1,0:T(8,128)(2,1)}, bf16[512,1024]{1,0:T(8,128)(2,1)}) custom-call(f32[128,32,128]{2,1,0:T(8,128)} %all-gather.3.cloned.1.call-done.col_hbm, bf16[1024,1024]{1,0:T(8,128)(2,1)} %get-tuple-element.23.low_hi_hbm, bf16[1024,1024]{1,0:T(8,128)(2,1)} %get-tuple-element.24.low_lo_hbm, ...), custom_call_target="tpu_custom_call" | custom-call | flops 199999995904 | bytes 9000000 | tf_op jit(solution)/shard_map/solve_columns/pallas_call | solution.py:318
  167.1 4.7 %all-to-all-done.3.own_hbm = f32[128,32,128]{2,1,0:T(8,128)} async-done(((f32[128,32,128]{2,1,0:T(8,128)}), f32[128,32,128]{2,1,0:T(8,128)}, u32[]{:S(2)}, u32[]{:S(2)}) %all-to-all-start.3) | async-done | bytes 2097184 | tf_op jit(solution)/shard_map/all_to_all | solution.py:488
  171.8 1.3 slice.112
  173.1 2.4 %collective-permute-start.4 = (f32[128,16,128]{2,1,0:T(8,128)S(1)}, f32[128,16,128]{2,1,0:T(8,128)S(1)}, u32[]{:S(2)}, u32[]{:S(2)}) collective-permute-start(f32[128,16,128]{2,1,0:T(8,128)S(1)} %slice.112), channel_id=1, source_target_pairs={{0,128},{128,0},{1,129},{129,1},{2,130},{130,2},{3,131},{131,3},{4... | collective-permute-start | bytes 3145736 | tf_op jit(solution)/shard_map/ppermute | solution.py:496
  175.5 2.3 %collective-permute-done.4.other_hbm = f32[128,16,128]{2,1,0:T(8,128)S(1)} collective-permute-done((f32[128,16,128]{2,1,0:T(8,128)S(1)}, f32[128,16,128]{2,1,0:T(8,128)S(1)}, u32[]{:S(2)}, u32[]{:S(2)}) %collective-permute-start.4) | collective-permute-done | bytes 1048608 | tf_op jit(solution)/shard_map/ppermute | solution.py:496
  178.8 13.6 %solve_and_update.1 = (f32[512,1024]{1,0:T(8,128)}, f32[2048,128]{1,0:T(8,128)}) custom-call(s32[3]{0:T(128)} %pad_add_fusion.1.where_ref, f32[128,1024]{1,0:T(8,128)} %get-tuple-element.20.top_hbm, f32[128,32,128]{2,1,0:T(8,128)} %all-to-all-done.3.own_hbm, f32[128,16,128]{2,1,0:T(8,128)} %copy-done.4, f32[2048,128]{1,0:T(8,128)} %bitcast.124, ...), custom_call_target="tpu_custom_call" | custom-call | flops 6000000000 | bytes 14000000 | tf_op jit(solution)/shard_map/solve_and_update/pallas_call | solution.py:441
  (73 shorter events, 9.0 us)
Async XLA Ops:
  7.2 5.4 %copy-start.2 = (f32[1,3,1,128,6,1,128]{6,5,4,3,2,1,0:T(1,128)S(1)}, f32[1,3,1,128,6,1,128]{6,5,4,3,2,1,0:T(1,128)}, u32[]{:S(2)}) copy-start(f32[1,3,1,128,6,1,128]{6,5,4,3,2,1,0:T(1,128)} %param.4) | copy-start | bytes 3538948
  9.3 4.4 %collective-permute-start = (f32[2,128,128]{2,1,0:T(8,128)}, f32[2,128,128]{2,1,0:T(8,128)S(1)}, u32[]{:S(2)}, u32[]{:S(2)}) collective-permute-start(f32[2,128,128]{2,1,0:T(8,128)} %slice_bitcast_fusion.4), channel_id=1, source_target_pairs={{0,128},{128,0},{1,129},{129,1},{2,130},{130,2},{3,131},{131,3},{4... | collective-permute-start | bytes 393224 | tf_op jit(solution)/shard_map/ppermute | solution.py:496
  15.3 14.0 %copy-start.3 = (s32[2,48]{1,0:T(2,128)S(1)}, s32[2,48]{1,0:T(2,128)}, u32[]{:S(2)}) copy-start(s32[2,48]{1,0:T(2,128)} %param.5) | copy-start | bytes 1156
  15.3 44.6 %all-to-all-start = ((f32[128,14,128]{2,1,0:T(8,128)}), f32[128,14,128]{2,1,0:T(8,128)S(1)}, u32[]{:S(2)}, u32[]{:S(2)}) async-start(f32[128,14,128]{2,1,0:T(8,128)} %copy.78), calls=%async_computation | async-start | bytes 2097152 | tf_op jit(solution)/shard_map/all_to_all | solution.py:488
  29.2 129.2 %all-gather.3.cloned.1.call-start = ((), (), s32[]{:S(2)}) async-start(), calls=%async_computation.4 | async-start | bytes 2228224 | tf_op jit(solution)/shard_map/all_gather | solution.py:555
  62.7 3.4 %collective-permute-start.1 = (f32[64,8,128]{2,1,0:T(8,128)S(1)}, f32[64,8,128]{2,1,0:T(8,128)S(1)}, u32[]{:S(2)}, u32[]{:S(2)}) collective-permute-start(f32[64,8,128]{2,1,0:T(8,128)S(1)} %fusion.6), channel_id=1, source_target_pairs={{0,128},{128,0},{1,129},{129,1},{2,130},{130,2},{3,131},{131,3},{4... | collective-permute-start | bytes 786440 | tf_op jit(solution)/shard_map/ppermute | solution.py:496
  82.8 23.3 %all-to-all-start.2 = ((f32[16,144,128]{2,1,0:T(8,128)}), f32[16,144,128]{2,1,0:T(8,128)S(1)}, u32[]{:S(2)}, u32[]{:S(2)}) async-start(f32[16,144,128]{2,1,0:T(8,128)} %broadcast_in_dim.62), calls=%async_computation.2 | async-start | bytes 2359296 | tf_op jit(solution)/shard_map/all_to_all | solution.py:558
  88.1 2.6 %collective-permute-start.2 = (f32[48,32,128]{2,1,0:T(8,128)S(1)}, f32[48,32,128]{2,1,0:T(8,128)S(1)}, u32[]{:S(2)}, u32[]{:S(2)}) collective-permute-start(f32[48,32,128]{2,1,0:T(8,128)S(1)} %get-tuple-element.44), channel_id=1, source_target_pairs={{0,128},{128,0},{1,129},{129,1},{2,130},{130,2},{3,131},{131,3},{4... | collective-permute-start | bytes 2359304 | tf_op jit(solution)/shard_map/ppermute | solution.py:496
  106.1 4.5 %copy-start = (f32[16,144,128]{2,1,0:T(8,128)}, f32[16,144,128]{2,1,0:T(8,128)S(1)}, u32[]{:S(2)}) copy-start(f32[16,144,128]{2,1,0:T(8,128)S(1)} %all-to-all-done.2.own_ref) | copy-start | bytes 3538948
  106.1 4.5 %collective-permute-start.3 = (f32[16,144,128]{2,1,0:T(8,128)S(1)}, f32[16,144,128]{2,1,0:T(8,128)S(1)}, u32[]{:S(2)}, u32[]{:S(2)}) collective-permute-start(f32[16,144,128]{2,1,0:T(8,128)S(1)} %all-to-all-done.2.own_ref), channel_id=1, source_target_pairs={{0,128},{128,0},{1,129},{129,1},{2,130},{130,2},{3,131},{131,3},{4... | collective-permute-start | bytes 3538952 | tf_op jit(solution)/shard_map/ppermute | solution.py:496
  110.6 1.0 copy-start.1
  111.7 60.1 %all-to-all-start.3 = ((f32[128,32,128]{2,1,0:T(8,128)}), f32[128,32,128]{2,1,0:T(8,128)}, u32[]{:S(2)}, u32[]{:S(2)}) async-start(f32[128,32,128]{2,1,0:T(8,128)} %bitcast.43), calls=%async_computation.3 | async-start | bytes 4194304 | tf_op jit(solution)/shard_map/all_to_all | solution.py:488
  173.1 4.7 %collective-permute-start.4 = (f32[128,16,128]{2,1,0:T(8,128)S(1)}, f32[128,16,128]{2,1,0:T(8,128)S(1)}, u32[]{:S(2)}, u32[]{:S(2)}) collective-permute-start(f32[128,16,128]{2,1,0:T(8,128)S(1)} %slice.112), channel_id=1, source_target_pairs={{0,128},{128,0},{1,129},{129,1},{2,130},{130,2},{3,131},{131,3},{4... | collective-permute-start | bytes 3145736 | tf_op jit(solution)/shard_map/ppermute | solution.py:496
  177.8 1.0 copy-start.4
Sparse Core Ops, SparseCore 0:
  81.5 53.1 all-gather.2
where the time goes:
time: 200 us; the launch traced here: 199 us
  Pallas kernels  64.3 us (32%)
  waiting for transfers between devices  55.8 us (28%)
  starting transfers between devices  35.7 us (18%)
  between operations  14.5 us (7%)
  blocking collectives  14 us (7%)
  local copies, waits for them, and re-layouts  10.4 us (5%)
  matrix products  3.36 us (2%)
    pallas_call x1, Pallas kernels, cholesky(): pl.pallas_call(cholesky_kernel, in_specs=[pl.BlockSpec(memory_space=pltpu...  39.3 us
    all_to_all x2, waiting for transfers between devices, to_chips(): return lax.all_to_all(x, ('row', 'col'), 0, 0)  35.1 us
    all_to_all x2, starting transfers between devices, to_chips(): return lax.all_to_all(x, ('row', 'col'), 0, 0)  21.4 us
    all_to_all x1, blocking collectives, per_device(): lax.all_to_all(jnp.concatenate([for_cols.reshape(NC, 32, BLK), triangle],...  14 us
    pallas_call x1, Pallas kernels, solve_and_update(): pl.pallas_call(solve_kernel, in_specs=[pl.BlockSpec(memory_space=pltpu.SM...  13.6 us
    all_to_all x1, waiting for transfers between devices, per_device(): lax.all_to_all(jnp.broadcast_to(lead[None], (GR, HALF * 8, BLK)), 'row',...  12.6 us
    ppermute x5, starting transfers between devices, swap_cores(): return lax.ppermute(x, 'sub', [(0, 1), (1, 0)])  10.6 us
    pallas_call x1, Pallas kernels, solve_columns(): pl.pallas_call(column_kernel, in_specs=[anywhere] * len(inputs), out_spec...  8.67 us
  transfers between devices with their start and end apart: 9, of which 8 were waited for; matrix products, arithmetic and copies ran while one was open for 2% of the time, Pallas kernels for 25%

commit v1 on v0

--- a/solution.py
+++ b/solution.py
@@ -31,9 +31,10 @@
 
 
 def dot_split(a, b):
-    left = jnp.concatenate([a[0], a[0], a[1]], 1)
-    right = jnp.concatenate([b[0], b[1], b[0]], 1)
-    return lax.dot_general(left, right, (((1,), (1,)), ((), ())), preferred_element_type=F32)
+    def dot(x, y):
+        return lax.dot_general(x, y, (((1,), (1,)), ((), ())), preferred_element_type=F32)
+
+    return dot(a[0], b[0]) + (dot(a[0], b[1]) + dot(a[1], b[0]))
 
 
 def split_rows(x):
@@ -148,7 +149,6 @@
 
 
 WIDE = 2 * BLK
-CHUNK = 512
 STRIP = 4 * BLK
 STEPS = P_SIZE // WIDE
 TRIANGLE = [(p, q) for q in range(NPB) for p in range(q, NPB)]
@@ -182,10 +182,10 @@
                 for p in range(n, NPB):
                     spot = TRIANGLE.index((p, n))
                     rows = slice(spot % HALF * 8, spot % HALF * 8 + 8)
-                    own = own_ref[:, rows, :].reshape(BLK, BLK)
-                    other = other_ref[:, rows, :].reshape(BLK, BLK)
+                    own, other = own_ref[:, rows, :], other_ref[:, rows, :]
                     is_own = first_core if spot < HALF else jnp.logical_not(first_core)
-                    panel[(p - n) * BLK : (p - n + 1) * BLK, :] = jnp.where(is_own, own, other)
+                    block = jnp.swapaxes(jnp.where(is_own, own, other), 0, 1).reshape(BLK, BLK)
+                    panel[(p - n) * BLK : (p - n + 1) * BLK, :] = block
                 if n:
                     panel[: P_SIZE - start, :] -= dot_full(
                         lower_ref[start:, :start], lower_ref[cols, :start], 1, 1
@@ -251,24 +251,20 @@
     )(where, own, other)
 
 
-def solve_strip(strip, lower, inverse, keep):
-    for m in range(STRIP // CHUNK):
-        rows = slice(m * CHUNK, (m + 1) * CHUNK)
-        high, low = [], []
-        for n in range(STEPS):
-            cols = slice(n * WIDE, (n + 1) * WIDE)
-            part = strip[rows, cols]
-            if n:
-                done = slice(0, n * WIDE)
-                part = part - dot_split(
-                    (jnp.concatenate(high, 1), jnp.concatenate(low, 1)),
-                    (lower[0][cols, done], lower[1][cols, done]),
-                )
-            part = dot_split(split(part), (inverse[0][n], inverse[1][n]))
-            hi, lo = split(part)
-            high.append(hi)
-            low.append(lo)
-            keep(rows, cols, part, hi, lo)
+def solve_strip(strip, lower, inverse, done_hi, done_lo, factor=None, ready=None):
+    for n in range(STEPS):
+        cols, done = slice(n * WIDE, (n + 1) * WIDE), slice(0, n * WIDE)
+        part = strip[:, cols]
+        if ready is not None:
+            ready(n)
+        if n:
+            part = part - dot_split(
+                (done_hi[:, done], done_lo[:, done]), (lower[0][cols, done], lower[1][cols, done])
+            )
+        part = dot_split(split(part), (inverse[0][n], inverse[1][n]))
+        if factor is not None:
+            factor[:, cols] = part
+        done_hi[:, cols], done_lo[:, cols] = split(part)
 
 
 def column_kernel(
@@ -299,17 +295,15 @@
         load.start()
     loads[0].wait()
     for b in range(4):
-        part = jnp.swapaxes(col_ref[:, b * NPB : (b + 1) * NPB, :], 0, 1)
+        part = jnp.swapaxes(col_ref[:, :, b * NPB : (b + 1) * NPB, :], 0, 1)
+        part = jnp.swapaxes(part.reshape(BLK, NPB, BLK), 0, 1)
         for q in range(NPB):
             cols = slice(q * BLK, (q + 1) * BLK)
             strip[b * BLK : (b + 1) * BLK, cols] = part[q]
     for load in loads[1:]:
         load.wait()
 
-    def keep(rows, cols, x, hi, lo):
-        col_hi[rows, cols], col_lo[rows, cols] = hi, lo
-
-    solve_strip(strip, (low_hi, low_lo), (inv_hi, inv_lo), keep)
+    solve_strip(strip, (low_hi, low_lo), (inv_hi, inv_lo), col_hi, col_lo)
 
 
 def solve_columns(col_strip, *factor_parts):
@@ -330,129 +324,215 @@
     )(*inputs)
 
 
-def solve_kernel(
-    where_ref,
-    top_hbm,
+def row_kernel(
     own_hbm,
-    other_hbm,
-    entry_hbm,
-    col_hi_hbm,
-    col_lo_hbm,
     low_hi_hbm,
     low_lo_hbm,
     inv_hi_hbm,
     inv_lo_hbm,
-    factor_hbm,
-    out_hbm,
-    top_ref,
+    factor_ref,
     own_ref,
-    other_ref,
-    entry_ref,
-    col_hi,
-    col_lo,
     low_hi,
     low_lo,
     inv_hi,
     inv_lo,
-    factor_ref,
-    out_ref,
     strip,
     row_hi,
     row_lo,
     sems,
 ):
-    first_core, grid_row, grid_col = where_ref[0] == 0, where_ref[1], where_ref[2]
     pairs = [
-        (own_hbm, own_ref),
-        (other_hbm, other_ref),
+        (own_hbm.at[:, 16:, :], own_ref),
         (inv_hi_hbm, inv_hi),
         (inv_lo_hbm, inv_lo),
-        (low_hi_hbm, low_hi),
-        (low_lo_hbm, low_lo),
-        (col_hi_hbm, col_hi),
-        (col_lo_hbm, col_lo),
-        (top_hbm, top_ref),
-        (entry_hbm, entry_ref),
     ]
+    for n in range(1, STEPS):
+        spot = (slice(n * WIDE, (n + 1) * WIDE), slice(0, n * WIDE))
+        pairs += [(low_hi_hbm.at[spot], low_hi.at[spot]), (low_lo_hbm.at[spot], low_lo.at[spot])]
     loads = [pltpu.make_async_copy(a, b, sems.at[n]) for n, (a, b) in enumerate(pairs)]
     for load in loads:
         load.start()
-    for load in loads[:2]:
-        load.wait()
+    loads[0].wait()
+    for h in range(2):
+        part = jnp.swapaxes(own_ref[:, h * NPB : (h + 1) * NPB, :], 0, 1)
+        for q in range(NPB):
+            strip[h * BLK : (h + 1) * BLK, q * BLK : (q + 1) * BLK] = part[q]
+
+    def ready(n):
+        for load in loads[1 + 2 * n : 3 + 2 * n]:
+            load.wait()
+
+    solve_strip(strip, (low_hi, low_lo), (inv_hi, inv_lo), row_hi, row_lo, factor_ref, ready)
+
+
+def solve_rows(rows_in, *factor_parts):
+    anywhere = pl.BlockSpec(memory_space=pl.ANY)
+    half = (STRIP // 2, P_SIZE)
+    return pl.pallas_call(
+        row_kernel,
+        in_specs=[anywhere] * 5,
+        out_specs=pl.BlockSpec(memory_space=pltpu.VMEM),
+        out_shape=jax.ShapeDtypeStruct(half, F32),
+        scratch_shapes=[pltpu.VMEM((BLK, 16, BLK), F32)]
+        + [pltpu.VMEM(x.shape, x.dtype) for x in factor_parts]
+        + [pltpu.VMEM(half, F32)]
+        + [pltpu.VMEM(half, jnp.bfloat16)] * 2
+        + [pltpu.SemaphoreType.DMA((9,))],
+        compiler_params=pltpu.CompilerParams(vmem_limit_bytes=60 * 2**20),
+        cost_estimate=pl.CostEstimate(
+            flops=2_000_000_000, bytes_accessed=5_000_000, transcendentals=0
+        ),
+        name="solve_rows",
+    )(rows_in, *factor_parts)
+
+
+def front_kernel(where_ref, sums_hbm, entry_ref, front_ref, sums_ref, sem):
+    grid_row, grid_col = where_ref[1], where_ref[2]
+    load = pltpu.make_async_copy(sums_hbm.at[:, :16, :], sums_ref, sem)
+    load.start()
+    load.wait()
     for b in range(4):
-        is_own = first_core if b < 2 else jnp.logical_not(first_core)
-        half = b % 2 * NPB
-        own, other = own_ref[:, 16 + half : 24 + half, :], other_ref[:, half : half + NPB, :]
-        picked = jnp.swapaxes(jnp.where(is_own, own, other), 0, 1)
-        for q in range(NPB):
-            strip[b * BLK : (b + 1) * BLK, q * BLK : (q + 1) * BLK] = picked[q]
-    for load in loads[2:6]:
-        load.wait()
-
-    def keep_row(rows, cols, x, hi, lo):
-        factor_ref[rows, cols] = x
-        row_hi[rows, cols], row_lo[rows, cols] = hi, lo
-
-    solve_strip(strip, (low_hi, low_lo), (inv_hi, inv_lo), keep_row)
-    for load in loads[6:]:
-        load.wait()
-
-    @pl.when(grid_row < NPB)
-    def _():
-        factor_ref[:BLK, :] = top_ref[...]
-
-    factor_store = pltpu.make_async_copy(factor_ref, factor_hbm, sems.at[10])
-    factor_store.start()
-    for b in range(4):
-        rows = slice(b * BLK, (b + 1) * BLK)
-        strip[rows, :STRIP] = dot_split(
-            (row_hi[rows, :], row_lo[rows, :]), (col_hi[...], col_lo[...])
-        )
         if b % 2 == 0:
-            all_sums = jnp.swapaxes(own_ref[:, b * 4 : b * 4 + 8, :], 0, 1)
+            blocks = jnp.swapaxes(sums_ref[:, b * 4 : b * 4 + 8, :], 0, 1)
         for d in range(4):
-            sums = all_sums[b % 2 * 4 + d]
+            sums = blocks[b % 2 * 4 + d]
             if b < d:
                 sums = sums.T
             elif b == d:
                 sums = jnp.where(grid_row >= grid_col, sums, sums.T)
-            spot = pl.ds(b * STRIP + d, BLK, stride=4)
-            block = entry_ref[spot, :] + sums
-            trail = strip[rows, d * BLK : (d + 1) * BLK]
+            entry = entry_ref[pl.ds(b * STRIP + d, BLK, stride=4), :]
+            front_ref[b * BLK : (b + 1) * BLK, d * BLK : (d + 1) * BLK] = entry + sums
+
+
+def assemble(where, rows_in, entries):
+    whole = pl.BlockSpec(memory_space=pltpu.VMEM)
+    return pl.pallas_call(
+        front_kernel,
+        in_specs=[
+            pl.BlockSpec(memory_space=pltpu.SMEM),
+            pl.BlockSpec(memory_space=pl.ANY),
+            whole,
+        ],
+        out_specs=whole,
+        out_shape=jax.ShapeDtypeStruct((STRIP, STRIP), F32),
+        scratch_shapes=[pltpu.VMEM((BLK, 16, BLK), F32), pltpu.SemaphoreType.DMA(())],
+        compiler_params=pltpu.CompilerParams(vmem_limit_bytes=60 * 2**20),
+        cost_estimate=pl.CostEstimate(
+            flops=1_000_000_000, bytes_accessed=4_000_000, transcendentals=0
+        ),
+        name="assemble",
+    )(where, rows_in, entries)
+
+
+def update_kernel(
+    where_ref,
+    own_hbm,
+    other_hbm,
+    col_hi_hbm,
+    col_lo_hbm,
+    front_hbm,
+    top_hbm,
+    factor_hbm,
+    out_hbm,
+    col_hi,
+    col_lo,
+    front_ref,
+    top_ref,
+    factor_ref,
+    out_ref,
+    product,
+    sems,
+):
+    first_core, grid_row, grid_col = where_ref[0] == 0, where_ref[1], where_ref[2]
+    pairs = [(col_hi_hbm, col_hi), (col_lo_hbm, col_lo), (front_hbm, front_ref), (top_hbm, top_ref)]
+    loads = [pltpu.make_async_copy(a, b, sems.at[n]) for n, (a, b) in enumerate(pairs)]
+    halves = factor_ref.at[: STRIP // 2], factor_ref.at[STRIP // 2 :]
+
+    def load_rows(first, second):
+        copies = [
+            pltpu.make_async_copy(first, halves[0], sems.at[4]),
+            pltpu.make_async_copy(second, halves[1], sems.at[5]),
+        ]
+        for copy in copies:
+            copy.start()
+        for load in loads:
+            load.start()
+        for copy in copies:
+            copy.wait()
+
+    @pl.when(first_core)
+    def _():
+        load_rows(own_hbm, other_hbm)
+
+    @pl.when(jnp.logical_not(first_core))
+    def _():
+        load_rows(other_hbm, own_hbm)
+
+    for load in loads:
+        load.wait()
+
+    @pl.when(grid_row < NPB)
+    def _():
+        factor_ref[:BLK, :] = top_ref[...]
+
+    factor_store = pltpu.make_async_copy(factor_ref, factor_hbm, sems.at[6])
+    factor_store.start()
+    product[...] = dot_split(split(factor_ref[...]), (col_hi[...], col_lo[...]))
+    for b in range(4):
+        for d in range(4):
+            rows, cols = slice(b * BLK, (b + 1) * BLK), slice(d * BLK, (d + 1) * BLK)
+            trail = product[rows, cols]
             if b == 0:
                 trail = jnp.where(grid_row >= NPB, trail, 0.0)
             if d == 0:
                 trail = jnp.where(grid_col >= NPB, trail, 0.0)
-            out_ref[spot, :] = block - trail
-    out_store = pltpu.make_async_copy(out_ref, out_hbm, sems.at[11])
+            out_ref[pl.ds(b * STRIP + d, BLK, stride=4), :] = front_ref[rows, cols] - trail
+    out_store = pltpu.make_async_copy(out_ref, out_hbm, sems.at[7])
     out_store.start()
     factor_store.wait()
     out_store.wait()
 
 
-def solve_and_update(where, top, own, other, entries, *solved):
-    bf16 = jnp.bfloat16
-    inputs = (top, own, other, entries, *solved)
+def update(where, own, other, columns, front, top):
+    inputs = (own, other, *columns, front, top)
     outputs = [
         jax.ShapeDtypeStruct((STRIP, P_SIZE), F32),
         jax.ShapeDtypeStruct((4 * STRIP, BLK), F32),
     ]
     anywhere = pl.BlockSpec(memory_space=pl.ANY)
     return pl.pallas_call(
-        solve_kernel,
+        update_kernel,
         in_specs=[pl.BlockSpec(memory_space=pltpu.SMEM)] + [anywhere] * len(inputs),
         out_specs=[anywhere] * 2,
         out_shape=outputs,
-        scratch_shapes=[pltpu.VMEM(x.shape, x.dtype) for x in (*inputs, *outputs)]
-        + [pltpu.VMEM((STRIP, P_SIZE), F32)]
-        + [pltpu.VMEM((STRIP, P_SIZE), bf16)] * 2
-        + [pltpu.SemaphoreType.DMA((12,))],
+        scratch_shapes=[pltpu.VMEM(x.shape, x.dtype) for x in (*inputs[2:], *outputs)]
+        + [pltpu.VMEM((STRIP, STRIP), F32), pltpu.SemaphoreType.DMA((8,))],
         compiler_params=pltpu.CompilerParams(vmem_limit_bytes=60 * 2**20),
         cost_estimate=pl.CostEstimate(
-            flops=6_000_000_000, bytes_accessed=14_000_000, transcendentals=0
+            flops=2_000_000_000, bytes_accessed=9_000_000, transcendentals=0
         ),
-        name="solve_and_update",
+        name="update",
     )(where, *inputs)
+
+
+def split_kernel(counts, child_ref, entry_ref, out_ref):
+    sources = [(child_ref, 6 * BLK * b + d, 6) for b, n in enumerate(counts) for d in range(n)]
+    sources += [(entry_ref, STRIP * b, 4) for b in range(4)]
+    for slot, (ref, start, stride) in enumerate(sources):
+        out_ref[pl.ds(slot, BLK, stride=16), :] = ref[pl.ds(start, BLK, stride=stride), :]
+
+
+def split_blocks(counts, child, entries):
+    whole = pl.BlockSpec(memory_space=pltpu.VMEM)
+    return pl.pallas_call(
+        functools.partial(split_kernel, counts),
+        in_specs=[whole] * 2,
+        out_specs=whole,
+        out_shape=jax.ShapeDtypeStruct((BLK * 16, BLK), F32),
+        compiler_params=pltpu.CompilerParams(vmem_limit_bytes=60 * 2**20),
+        cost_estimate=pl.CostEstimate(flops=0, bytes_accessed=3_000_000, transcendentals=0),
+        name="split_blocks",
+    )(child, entries)
 
 
 def pack_kernel(inverse_map_ref, own_ref, other_ref, panel_ref, out_ref):
@@ -463,12 +543,12 @@
             spot = inverse_map_ref[k, p]
             total = total + jnp.where(spot >= 0, child[jnp.maximum(spot, 0)], 0.0)
         for d in range(4):
-            out_ref[pl.ds(r * 256 + b * 4 + d, NC, stride=32), :] = total[d * NC : (d + 1) * NC]
+            out_ref[pl.ds(r * 32 + b * 4 + d, NC, stride=GR * 32), :] = total[d * NC : (d + 1) * NC]
     for h in range(2):
         for r in range(GR):
             rows = panel_ref[h, r]
             for c in range(NC):
-                out_ref[pl.ds(r * 256 + c * 32 + 16 + h * 8, NPB), :] = rows
+                out_ref[pl.ds((c * GR + r) * 32 + 16 + h * 8, NPB), :] = rows
 
 
 def pack(inverse_maps, own, other, panel):
@@ -485,7 +565,7 @@
 
 
 def to_chips(x):
-    return lax.all_to_all(x, ("row", "col"), 0, 0)
+    return lax.all_to_all(x, ("col", "row"), 0, 0)
 
 
 def after(x, earlier):
@@ -507,24 +587,19 @@
     blocks = jnp.arange(FB, dtype=jnp.int32)
     where = jnp.stack([my_sub, my_row, my_sub * NC + my_col]).astype(jnp.int32)
 
-    entry_panel = entries[:, :, 0, :]
-    from_first = swap_cores(entry_panel[2:])
-    entry_half = jnp.where(my_sub == 0, entry_panel[:2], from_first)
     counts = [2 * b + 2 for b in range(3)]
-    slices_out = jnp.concatenate(
-        [child_own[b, :, :count, :] for b, count in enumerate(counts)]
-        + [entry_half.transpose(1, 0, 2)],
-        1,
-    )
-    slices_in = to_chips(slices_out).reshape(GR, NC, 14, BLK)
+    entries = entries.reshape(4 * STRIP, BLK)
+    slices_out = split_blocks(counts, child_own.reshape(18 * BLK, BLK), entries)
+    slices_out = slices_out.reshape(CHIPS, 16, BLK)
+    slices_in = to_chips(slices_out).reshape(NC, GR, 16, BLK)
     lower_child, start = [], 0
     for count in counts:
-        part = slices_in[:, :, start : start + count].transpose(0, 2, 1, 3)
+        part = slices_in[:, :, start : start + count].transpose(1, 2, 0, 3)
         part = jnp.pad(part, ((0, 0), (0, 6 - count), (0, 0), (0, 0)))
         lower_child.append(part.reshape(GR, UB, BLK))
         start += count
     lower_child = jnp.concatenate(lower_child, 0)
-    entry_rows = slices_in[:, :, start:].transpose(2, 0, 1, 3).reshape(FB // 2, NPB, BLK)
+    entry_rows = slices_in[:, :, start:].transpose(2, 1, 0, 3).reshape(FB, NPB, BLK)
 
     row_pick = (own_map[None, :] == blocks[:, None]).astype(F32)
     col_pick = (own_map[None, :NPB] == blocks[:NPB, None]).astype(F32)
@@ -533,14 +608,7 @@
     )
     child_panel = lower_child[:, :NPB].reshape(UB * NPB, BLK)
     placed = dot_full(both_pick, child_panel, 1, 0).reshape(FB, NPB, BLK)
-    no_rows = jnp.zeros_like(entry_rows)
-    placed = placed + jnp.concatenate(
-        [
-            jnp.where(my_sub == 0, entry_rows, no_rows),
-            jnp.where(my_sub == 0, no_rows, entry_rows),
-        ],
-        0,
-    )
+    placed = placed + jnp.where(my_sub == 0, entry_rows, 0.0)
     panel_rows = placed + swap_cores(placed)
 
     by_grid = panel_rows.reshape(4, 2, NC, NPB, BLK)
@@ -552,7 +620,6 @@
         jnp.concatenate([for_cols.reshape(NC, 32, BLK), triangle], 1), "col", 0, 0
     )
     col_part = along_col[:, :32]
-    col_strip = lax.all_gather(col_part, "row", axis=0)
     lead = along_col[:, 32:].transpose(1, 0, 2).reshape(HALF * 8, BLK)
     lead = after(lead, col_part)
     lead = lax.all_to_all(jnp.broadcast_to(lead[None], (GR, HALF * 8, BLK)), "row", 0, 0)
@@ -579,20 +646,16 @@
     rows_out = pack(inverse_maps, kept, arrived, for_rows).reshape(CHIPS, 32, BLK)
     lead, rows_out = lax.optimization_barrier((lead, rows_out))
     other_lead = swap_cores(lead)
-    rows_in = to_chips(after(rows_out, other_lead))
+    col_strip = lax.all_gather(after(col_part, lead), "row", axis=0)
+    rows_in = to_chips(rows_out)
 
     *factor_parts, top = cholesky(where, lead, other_lead)
-    columns = solve_columns(col_strip.reshape(CHIPS, 32, BLK), *factor_parts)
+    columns = solve_columns(col_strip, *factor_parts)
     rows_in = after(rows_in, columns[0])
-    factor, updated = solve_and_update(
-        where,
-        top,
-        rows_in,
-        swap_cores(rows_in[:, 16:]),
-        entries.reshape(4 * STRIP, BLK),
-        *columns,
-        *factor_parts,
-    )
+    own_rows = solve_rows(rows_in, *factor_parts)
+    other_rows = swap_cores(own_rows)
+    front = assemble(where, rows_in, after(entries, own_rows))
+    factor, updated = update(where, own_rows, other_rows, columns, front, top)
     updated = updated.reshape(4, 1, BLK, 4, 1, BLK)
     return updated, factor.reshape(4, 1, BLK, P_SIZE)
 

time: 200 us -> 190 us (0.950)
  blocking collectives: 14 us -> 0 us
  local copies, waits for them, and re-layouts: 10.4 us -> 5.02 us
  Pallas kernels: 64.3 us -> 69.3 us
  starting transfers between devices: 35.7 us -> 39.6 us
    all_to_all x1 -> x0, blocking collectives: 14 us -> none  [per_device(): lax.all_to_all(jnp.concatenate([for_cols.reshape(NC, 32, BLK), triangle],...]
    all_to_all x2 -> x3, starting transfers between devices: 21.4 us -> 27.4 us  [the longest x2 24 us: to_chips(): return lax.all_to_all(x, ('col', 'row'), 0, 0)]
    ppermute x5 -> x4, waiting for transfers between devices: 8.12 us -> 2.94 us  [swap_cores(): return lax.ppermute(x, 'sub', [(0, 1), (1, 0)])]
    pallas_call x1 -> x4, Pallas kernels: 13.6 us -> 18.5 us  [the longest x1 6.18 us: update(): pl.pallas_call(update_kernel, in_specs=[pl.BlockSpec(memory_space=pltpu.S...]
    all_to_all x2 -> x3, waiting for transfers between devices: 35.1 us -> 39.5 us  [the longest x2 28.3 us: to_chips(): return lax.all_to_all(x, ('col', 'row'), 0, 0)]
    ppermute x5 -> x4, starting transfers between devices: 10.6 us -> 8.42 us  [swap_cores(): return lax.ppermute(x, 'sub', [(0, 1), (1, 0)])]
    all_gather x1, waiting for transfers between devices: 0.01 us -> 2.05 us  [per_device(): col_strip = lax.all_gather(after(col_part, lead), 'row', axis=0)]
    unnamed x19 -> x15, local copies, waits for them, and re-layouts: 4.03 us -> 2.14 us
  transfers between devices with their start and end apart: 9 -> 9, of which waited for: 8 -> 6; matrix products, arithmetic and copies ran while one was open for 2% -> 2% of each run, Pallas kernels for 25% -> 29%
where the time goes in v1:
time: 190 us
  Pallas kernels  69.3 us (36%)
  waiting for transfers between devices  55.9 us (29%)
  starting transfers between devices  39.6 us (21%)
  between operations  14.4 us (8%)
  local copies, waits for them, and re-layouts  5.02 us (3%)
  matrix products  3.35 us (2%)
  other arithmetic  2 us (1%)
    pallas_call x1, Pallas kernels, cholesky(): pl.pallas_call(cholesky_kernel, in_specs=[pl.BlockSpec(memory_space=pltpu...  39.4 us
    all_to_all x2, waiting for transfers between devices, to_chips(): return lax.all_to_all(x, ('col', 'row'), 0, 0)  28.3 us
    all_to_all x2, starting transfers between devices, to_chips(): return lax.all_to_all(x, ('col', 'row'), 0, 0)  24 us
    all_to_all x1, waiting for transfers between devices, per_device(): lax.all_to_all(jnp.broadcast_to(lead[None], (GR, HALF * 8, BLK)), 'row',...  11.4 us
    all_to_all x1, waiting for transfers between devices, per_device(): lax.all_to_all(jnp.concatenate([for_cols.reshape(NC, 32, BLK), triangle],...  11.2 us
    pallas_call x1, Pallas kernels, solve_columns(): pl.pallas_call(column_kernel, in_specs=[anywhere] * len(inputs), out_spec...  8.67 us
    ppermute x4, starting transfers between devices, swap_cores(): return lax.ppermute(x, 'sub', [(0, 1), (1, 0)])  8.42 us
    pallas_call x1, Pallas kernels, update(): pl.pallas_call(update_kernel, in_specs=[pl.BlockSpec(memory_space=pltpu.S...  6.18 us
  transfers between devices with their start and end apart: 9, of which 6 were waited for; matrix products, arithmetic and copies ran while one was open for 2% of the time, Pallas kernels for 29%

profile of v1, /device:TPU:1, one launch (start us, length us, event | category | flops | bytes accessed | tf_op | source)
XLA Modules:
  0.0 189.6 jit_solution(15162016759130459728)
XLA Ops:
  7.2 3.1 %split_blocks.1 = f32[2048,128]{1,0:T(8,128)} custom-call(f32[2304,128]{1,0:T(8,128)} %bitcast.99, f32[2048,128]{1,0:T(8,128)} %bitcast.93), custom_call_target="tpu_custom_call" | custom-call | bytes 3000000 | tf_op jit(solution)/shard_map/split_blocks/pallas_call | solution.py:527
  10.3 16.5 %all-to-all-start = ((f32[128,16,128]{2,1,0:T(8,128)}), f32[128,16,128]{2,1,0:T(8,128)S(1)}, u32[]{:S(2)}, u32[]{:S(2)}) async-start(f32[128,16,128]{2,1,0:T(8,128)} %bitcast.95), calls=%async_computation | async-start | bytes 2097152 | tf_op jit(solution)/shard_map/all_to_all | solution.py:568
  27.0 28.3 %all-to-all-done = f32[128,16,128]{2,1,0:T(8,128)S(1)} async-done(((f32[128,16,128]{2,1,0:T(8,128)}), f32[128,16,128]{2,1,0:T(8,128)S(1)}, u32[]{:S(2)}, u32[]{:S(2)}) %all-to-all-start) | async-done | bytes 1048608 | tf_op jit(solution)/shard_map/all_to_all | solution.py:568
  56.1 1.9 %fusion.6 = f32[64,8,128]{2,1,0:T(8,128)S(1)} fusion(f32[64,8,128]{2,1,0:T(8,128)S(1)} %bitcast.105, f32[8,8]{0,1:T(8,128)S(1)} %compare_convert_fusion, f32[64,48]{1,0:T(8,128)S(1)} %copy.49, f32[48,48,128]{2,0,1:T(8,128)S(1)} %pad_maximum_fusion), kind=kOutput, calls=%fused_computation.8 | convolution fusion | flops 302252032 | bytes 757760 | tf_op jit(solution)/shard_map/dot_general | solution.py:23
  58.0 3.6 %collective-permute-start = (f32[64,8,128]{2,1,0:T(8,128)S(1)}, f32[64,8,128]{2,1,0:T(8,128)S(1)}, u32[]{:S(2)}, u32[]{:S(2)}) collective-permute-start(f32[64,8,128]{2,1,0:T(8,128)S(1)} %fusion.6), channel_id=1, source_target_pairs={{0,128},{128,0},{1,129},{129,1},{2,130},{130,2},{3,131},{131,3},{4... | collective-permute-start | bytes 786440 | tf_op jit(solution)/shard_map/ppermute | solution.py:576
  61.6 1.2 collective-permute-done
  64.0 3.4 %all-to-all-start.1 = ((f32[8,50,128]{2,1,0:T(8,128)}), f32[8,50,128]{2,1,0:T(8,128)S(1)}, u32[]{:S(2)}, u32[]{:S(2)}) async-start(f32[8,50,128]{2,1,0:T(8,128)} %pad_maximum_fusion.1), calls=%async_computation.1 | async-start | bytes 458752 | tf_op jit(solution)/shard_map/all_to_all | solution.py:619
  67.7 11.2 %all-to-all-done.1 = f32[8,50,128]{2,1,0:T(8,128)S(1)} async-done(((f32[8,50,128]{2,1,0:T(8,128)}), f32[8,50,128]{2,1,0:T(8,128)S(1)}, u32[]{:S(2)}, u32[]{:S(2)}) %all-to-all-start.1) | async-done | bytes 204832 | tf_op jit(solution)/shard_map/all_to_all | solution.py:619
  79.6 1.1 broadcast_in_dim.63
  80.7 3.7 %all-to-all-start.2 = ((f32[16,144,128]{2,1,0:T(8,128)}), f32[16,144,128]{2,1,0:T(8,128)S(1)}, u32[]{:S(2)}, u32[]{:S(2)}) async-start(f32[16,144,128]{2,1,0:T(8,128)} %broadcast_in_dim.63), calls=%async_computation.2 | async-start | bytes 2359296 | tf_op jit(solution)/shard_map/all_to_all | solution.py:625
  84.5 1.4 convolution_bitcast_fusion
  86.8 1.8 collective-permute-done.1.other_ref
  88.6 2.8 %pack.1 = f32[4096,128]{1,0:T(8,128)} custom-call(s32[2,64]{1,0:T(2,128)S(1)} %select_reduce_fusion.inverse_map_ref, f32[48,32,128]{2,1,0:T(8,128)S(1)} %get-tuple-element.45.own_ref, f32[48,32,128]{2,1,0:T(8,128)S(1)} %collective-permute-done.1.other_ref, f32[2,16,8,128]{3,2,1,0:T(8,128)S(1)} %dynamic-slice_bitcast_fusion.panel_ref), custom_call_target="tpu_custom_call" | custom-call | bytes 8000000 | tf_op jit(solution)/shard_map/pack/pallas_call | solution.py:556
  91.4 11.4 %all-to-all-done.2.own_ref = f32[16,144,128]{2,1,0:T(8,128)S(1)} async-done(((f32[16,144,128]{2,1,0:T(8,128)}), f32[16,144,128]{2,1,0:T(8,128)S(1)}, u32[]{:S(2)}, u32[]{:S(2)}) %all-to-all-start.2) | async-done | bytes 1179680 | tf_op jit(solution)/shard_map/all_to_all | solution.py:625
  102.8 2.1 %collective-permute-start.2 = (f32[16,144,128]{2,1,0:T(8,128)S(1)}, f32[16,144,128]{2,1,0:T(8,128)S(1)}, u32[]{:S(2)}, u32[]{:S(2)}) collective-permute-start(f32[16,144,128]{2,1,0:T(8,128)S(1)} %all-to-all-done.2.own_ref), channel_id=1, source_target_pairs={{0,128},{128,0},{1,129},{129,1},{2,130},{130,2},{3,131},{131,3},{4... | collective-permute-start | bytes 3538952 | tf_op jit(solution)/shard_map/ppermute | solution.py:576
  105.6 7.5 %all-to-all-start.3 = ((f32[128,32,128]{2,1,0:T(8,128)}), f32[128,32,128]{2,1,0:T(8,128)}, u32[]{:S(2)}, u32[]{:S(2)}) async-start(f32[128,32,128]{2,1,0:T(8,128)} %bitcast.36), calls=%async_computation.3 | async-start | bytes 4194304 | tf_op jit(solution)/shard_map/all_to_all | solution.py:568
  113.1 1.0 copy-done.1
  114.2 39.4 %cholesky.1 = (bf16[1024,1024]{1,0:T(8,128)(2,1)}, bf16[1024,1024]{1,0:T(8,128)(2,1)}, bf16[4,256,256]{2,1,0:T(8,128)(2,1)}, bf16[4,256,256]{2,1,0:T(8,128)(2,1)}, f32[128,1024]{1,0:T(8,128)}) custom-call(s32[3]{0:T(128)} %pad_add_fusion.1.where_ref, f32[16,144,128]{2,1,0:T(8,128)} %copy-done, f32[16,144,128]{2,1,0:T(8,128)} %copy-done.1), custom_call_target="tpu_custom_call" | custom-call | flops 1 | bytes 1 | tf_op jit(solution)/shard_map/cholesky/pallas_call | solution.py:233
  153.5 2.1 %all-gather.3.cloned.1.call-done = f32[128,32,128]{2,1,0:T(8,128)} async-done(((f32[8,32,128]{2,1,0:T(8,128)}), f32[128,32,128]{2,1,0:T(8,128)}) %all-gather.3.cloned.1.call-update) | async-done | bytes 2097168 | tf_op jit(solution)/shard_map/all_gather | solution.py:649
  155.6 8.7 %solve_columns.1 = (bf16[512,1024]{1,0:T(8,128)(2,1)}, bf16[512,1024]{1,0:T(8,128)(2,1)}) custom-call(f32[16,8,32,128]{3,2,1,0:T(8,128)} %bitcast.116, bf16[1024,1024]{1,0:T(8,128)(2,1)} %get-tuple-element.23.low_hi_hbm, bf16[1024,1024]{1,0:T(8,128)(2,1)} %get-tuple-element.24.low_lo_hbm, bf16[4,256,256]{2,1,0:T(8,128)(2,1)} %get-tuple-element.25.inv_hi_hbm, ...), custom_call_target="tpu_custom_call" | custom-call | flops 199999995904 | bytes 9000000 | tf_op jit(solution)/shard_map/solve_columns/pallas_call | solution.py:312
  164.3 5.5 %solve_rows.1.own_hbm = f32[256,1024]{1,0:T(8,128)} custom-call(f32[128,32,128]{2,1,0:T(8,128)} %all-to-all-done.3.own_hbm.sums_hbm, bf16[1024,1024]{1,0:T(8,128)(2,1)} %get-tuple-element.23.low_hi_hbm, bf16[1024,1024]{1,0:T(8,128)(2,1)} %get-tuple-element.24.low_lo_hbm, bf16[4,256,256]{2,1,0:T(8,128)(2,1)} %get-tuple-element.25.inv_hi_hbm, ...), custom_call_target="tpu_custom_call" | custom-call | flops 2000000000 | bytes 5000000 | tf_op jit(solution)/shard_map/solve_rows/pallas_call | solution.py:371
  169.8 2.0 %collective-permute-start.3 = (f32[256,1024]{1,0:T(8,128)}, f32[256,1024]{1,0:T(8,128)S(1)}, u32[]{:S(2)}, u32[]{:S(2)}) collective-permute-start(f32[256,1024]{1,0:T(8,128)} %solve_rows.1.own_hbm), channel_id=1, source_target_pairs={{0,128},{128,0},{1,129},{129,1},{2,130},{130,2},{3,131},{131,3},{4... | collective-permute-start | bytes 3145736 | tf_op jit(solution)/shard_map/ppermute | solution.py:576
  171.8 3.7 %assemble.1.front_hbm = f32[512,512]{1,0:T(8,128)} custom-call(s32[3]{0:T(128)} %pad_add_fusion.1.where_ref, f32[128,32,128]{2,1,0:T(8,128)} %all-to-all-done.3.own_hbm.sums_hbm, f32[2048,128]{1,0:T(8,128)} %bitcast.94), custom_call_target="tpu_custom_call" | custom-call | flops 1000000000 | bytes 4000000 | tf_op jit(solution)/shard_map/assemble/pallas_call | solution.py:409
  176.6 6.2 %update.1 = (f32[512,1024]{1,0:T(8,128)}, f32[2048,128]{1,0:T(8,128)}) custom-call(s32[3]{0:T(128)} %pad_add_fusion.1.where_ref, f32[256,1024]{1,0:T(8,128)} %solve_rows.1.own_hbm, f32[256,1024]{1,0:T(8,128)} %copy-done.3, bf16[512,1024]{1,0:T(8,128)(2,1)} %get-tuple-element.27.col_hi_hbm, bf16[512,1024]{1,0:T(8,128)(2,1)} %get-tuple-element.29.col_lo_hbm, ...), custom_call_target="tpu_custom_call" | custom-call | flops 2000000000 | bytes 9000000 | tf_op jit(solution)/shard_map/update/pallas_call | solution.py:503
  (63 shorter events, 5.6 us)
Async XLA Ops:
  10.3 16.5 %copy-start.2 = (s32[2,48]{1,0:T(2,128)S(1)}, s32[2,48]{1,0:T(2,128)}, u32[]{:S(2)}) copy-start(s32[2,48]{1,0:T(2,128)} %param.5) | copy-start | bytes 1156
  10.3 45.1 %all-to-all-start = ((f32[128,16,128]{2,1,0:T(8,128)}), f32[128,16,128]{2,1,0:T(8,128)S(1)}, u32[]{:S(2)}, u32[]{:S(2)}) async-start(f32[128,16,128]{2,1,0:T(8,128)} %bitcast.95), calls=%async_computation | async-start | bytes 2097152 | tf_op jit(solution)/shard_map/all_to_all | solution.py:568
  58.0 4.8 %collective-permute-start = (f32[64,8,128]{2,1,0:T(8,128)S(1)}, f32[64,8,128]{2,1,0:T(8,128)S(1)}, u32[]{:S(2)}, u32[]{:S(2)}) collective-permute-start(f32[64,8,128]{2,1,0:T(8,128)S(1)} %fusion.6), channel_id=1, source_target_pairs={{0,128},{128,0},{1,129},{129,1},{2,130},{130,2},{3,131},{131,3},{4... | collective-permute-start | bytes 786440 | tf_op jit(solution)/shard_map/ppermute | solution.py:576
  64.0 14.9 %all-to-all-start.1 = ((f32[8,50,128]{2,1,0:T(8,128)}), f32[8,50,128]{2,1,0:T(8,128)S(1)}, u32[]{:S(2)}, u32[]{:S(2)}) async-start(f32[8,50,128]{2,1,0:T(8,128)} %pad_maximum_fusion.1), calls=%async_computation.1 | async-start | bytes 458752 | tf_op jit(solution)/shard_map/all_to_all | solution.py:619
  80.7 22.1 %all-to-all-start.2 = ((f32[16,144,128]{2,1,0:T(8,128)}), f32[16,144,128]{2,1,0:T(8,128)S(1)}, u32[]{:S(2)}, u32[]{:S(2)}) async-start(f32[16,144,128]{2,1,0:T(8,128)} %broadcast_in_dim.63), calls=%async_computation.2 | async-start | bytes 2359296 | tf_op jit(solution)/shard_map/all_to_all | solution.py:625
  84.4 71.2 %all-gather.3.cloned.1.call-start = ((), (), s32[]{:S(2)}) async-start(), calls=%async_computation.4 | async-start | bytes 2228224 | tf_op jit(solution)/shard_map/all_gather | solution.py:649
  86.1 2.6 %collective-permute-start.1 = (f32[48,32,128]{2,1,0:T(8,128)S(1)}, f32[48,32,128]{2,1,0:T(8,128)S(1)}, u32[]{:S(2)}, u32[]{:S(2)}) collective-permute-start(f32[48,32,128]{2,1,0:T(8,128)S(1)} %get-tuple-element.44), channel_id=1, source_target_pairs={{0,128},{128,0},{1,129},{129,1},{2,130},{130,2},{3,131},{131,3},{4... | collective-permute-start | bytes 2359304 | tf_op jit(solution)/shard_map/ppermute | solution.py:576
  102.8 2.8 %copy-start = (f32[16,144,128]{2,1,0:T(8,128)}, f32[16,144,128]{2,1,0:T(8,128)S(1)}, u32[]{:S(2)}) copy-start(f32[16,144,128]{2,1,0:T(8,128)S(1)} %all-to-all-done.2.own_ref) | copy-start | bytes 3538948
  102.8 10.3 %collective-permute-start.2 = (f32[16,144,128]{2,1,0:T(8,128)S(1)}, f32[16,144,128]{2,1,0:T(8,128)S(1)}, u32[]{:S(2)}, u32[]{:S(2)}) collective-permute-start(f32[16,144,128]{2,1,0:T(8,128)S(1)} %all-to-all-done.2.own_ref), channel_id=1, source_target_pairs={{0,128},{128,0},{1,129},{129,1},{2,130},{130,2},{3,131},{131,3},{4... | collective-permute-start | bytes 3538952 | tf_op jit(solution)/shard_map/ppermute | solution.py:576
  105.6 58.7 %all-to-all-start.3 = ((f32[128,32,128]{2,1,0:T(8,128)}), f32[128,32,128]{2,1,0:T(8,128)}, u32[]{:S(2)}, u32[]{:S(2)}) async-start(f32[128,32,128]{2,1,0:T(8,128)} %bitcast.36), calls=%async_computation.3 | async-start | bytes 4194304 | tf_op jit(solution)/shard_map/all_to_all | solution.py:568
  113.1 1.0 copy-start.1
  169.8 5.8 %collective-permute-start.3 = (f32[256,1024]{1,0:T(8,128)}, f32[256,1024]{1,0:T(8,128)S(1)}, u32[]{:S(2)}, u32[]{:S(2)}) collective-permute-start(f32[256,1024]{1,0:T(8,128)} %solve_rows.1.own_hbm), channel_id=1, source_target_pairs={{0,128},{128,0},{1,129},{129,1},{2,130},{130,2},{3,131},{131,3},{4... | collective-permute-start | bytes 3145736 | tf_op jit(solution)/shard_map/ppermute | solution.py:576
  175.6 1.0 copy-start.3
Sparse Core Ops, SparseCore 0:
  102.9 52.6 all-gather.2

commit v2 on v1

--- a/solution.py
+++ b/solution.py
@@ -212,7 +212,7 @@
     top_ref[...] = lower_ref[
         pl.ds(pl.multiple_of(jnp.minimum(grid_row, NPB - 1) * BLK, BLK), BLK), :
     ]
-    low_hi[...], low_lo[...] = split(lower_ref[...])
+    low_hi[...], low_lo[...] = split(lower_ref[WIDE:, : P_SIZE - WIDE])
     for n in range(STEPS):
         a, b = inverse_ref[2 * n], inverse_ref[2 * n + 1]
         mid = lower_ref[(2 * n + 1) * BLK : (2 * n + 2) * BLK, 2 * n * BLK : (2 * n + 1) * BLK]
@@ -234,7 +234,7 @@
         cholesky_kernel,
         in_specs=[pl.BlockSpec(memory_space=pltpu.SMEM), whole, whole],
         out_specs=[whole] * 5,
-        out_shape=[jax.ShapeDtypeStruct((P_SIZE, P_SIZE), bf16)] * 2
+        out_shape=[jax.ShapeDtypeStruct((P_SIZE - WIDE, P_SIZE - WIDE), bf16)] * 2
         + [jax.ShapeDtypeStruct((STEPS, WIDE, WIDE), bf16)] * 2
         + [jax.ShapeDtypeStruct((BLK, P_SIZE), F32)],
         scratch_shapes=[
@@ -254,17 +254,34 @@
 def solve_strip(strip, lower, inverse, done_hi, done_lo, factor=None, ready=None):
     for n in range(STEPS):
         cols, done = slice(n * WIDE, (n + 1) * WIDE), slice(0, n * WIDE)
+        above = slice((n - 1) * WIDE, n * WIDE)
         part = strip[:, cols]
         if ready is not None:
             ready(n)
         if n:
             part = part - dot_split(
-                (done_hi[:, done], done_lo[:, done]), (lower[0][cols, done], lower[1][cols, done])
+                (done_hi[:, done], done_lo[:, done]), (lower[0][above, done], lower[1][above, done])
             )
         part = dot_split(split(part), (inverse[0][n], inverse[1][n]))
         if factor is not None:
             factor[:, cols] = part
         done_hi[:, cols], done_lo[:, cols] = split(part)
+
+
+def start_loads(strip_hbm, strip_ref, parts, sems):
+    pairs = [(strip_hbm, strip_ref), *parts[2:]]
+    for n in range(1, STEPS):
+        spot = (slice((n - 1) * WIDE, n * WIDE), slice(0, n * WIDE))
+        pairs += [(source.at[spot], target.at[spot]) for source, target in parts[:2]]
+    loads = [pltpu.make_async_copy(a, b, sems.at[n]) for n, (a, b) in enumerate(pairs)]
+    for load in loads:
+        load.start()
+
+    def ready(n):
+        for load in loads[1 + 2 * n : 3 + 2 * n]:
+            load.wait()
+
+    return loads[0], ready
 
 
 def column_kernel(
@@ -283,27 +300,16 @@
     strip,
     sems,
 ):
-    pairs = [
-        (col_hbm, col_ref),
-        (inv_hi_hbm, inv_hi),
-        (inv_lo_hbm, inv_lo),
-        (low_hi_hbm, low_hi),
-        (low_lo_hbm, low_lo),
-    ]
-    loads = [pltpu.make_async_copy(a, b, sems.at[n]) for n, (a, b) in enumerate(pairs)]
-    for load in loads:
-        load.start()
-    loads[0].wait()
+    parts = ((low_hi_hbm, low_hi), (low_lo_hbm, low_lo), (inv_hi_hbm, inv_hi), (inv_lo_hbm, inv_lo))
+    first, ready = start_loads(col_hbm, col_ref, parts, sems)
+    first.wait()
     for b in range(4):
         part = jnp.swapaxes(col_ref[:, :, b * NPB : (b + 1) * NPB, :], 0, 1)
         part = jnp.swapaxes(part.reshape(BLK, NPB, BLK), 0, 1)
         for q in range(NPB):
             cols = slice(q * BLK, (q + 1) * BLK)
             strip[b * BLK : (b + 1) * BLK, cols] = part[q]
-    for load in loads[1:]:
-        load.wait()
-
-    solve_strip(strip, (low_hi, low_lo), (inv_hi, inv_lo), col_hi, col_lo)
+    solve_strip(strip, (low_hi, low_lo), (inv_hi, inv_lo), col_hi, col_lo, None, ready)
 
 
 def solve_columns(col_strip, *factor_parts):
@@ -315,7 +321,7 @@
         out_specs=[pl.BlockSpec(memory_space=pltpu.VMEM)] * 2,
         out_shape=[jax.ShapeDtypeStruct((STRIP, P_SIZE), jnp.bfloat16)] * 2,
         scratch_shapes=[pltpu.VMEM(x.shape, x.dtype) for x in inputs]
-        + [pltpu.VMEM((STRIP, P_SIZE), F32), pltpu.SemaphoreType.DMA((len(inputs),))],
+        + [pltpu.VMEM((STRIP, P_SIZE), F32), pltpu.SemaphoreType.DMA((9,))],
         compiler_params=pltpu.CompilerParams(vmem_limit_bytes=60 * 2**20),
         cost_estimate=pl.CostEstimate(
             flops=200_000_000_000, bytes_accessed=9_000_000, transcendentals=0
@@ -341,26 +347,13 @@
     row_lo,
     sems,
 ):
-    pairs = [
-        (own_hbm.at[:, 16:, :], own_ref),
-        (inv_hi_hbm, inv_hi),
-        (inv_lo_hbm, inv_lo),
-    ]
-    for n in range(1, STEPS):
-        spot = (slice(n * WIDE, (n + 1) * WIDE), slice(0, n * WIDE))
-        pairs += [(low_hi_hbm.at[spot], low_hi.at[spot]), (low_lo_hbm.at[spot], low_lo.at[spot])]
-    loads = [pltpu.make_async_copy(a, b, sems.at[n]) for n, (a, b) in enumerate(pairs)]
-    for load in loads:
-        load.start()
-    loads[0].wait()
+    parts = ((low_hi_hbm, low_hi), (low_lo_hbm, low_lo), (inv_hi_hbm, inv_hi), (inv_lo_hbm, inv_lo))
+    first, ready = start_loads(own_hbm.at[:, 16:, :], own_ref, parts, sems)
+    first.wait()
     for h in range(2):
         part = jnp.swapaxes(own_ref[:, h * NPB : (h + 1) * NPB, :], 0, 1)
         for q in range(NPB):
             strip[h * BLK : (h + 1) * BLK, q * BLK : (q + 1) * BLK] = part[q]
-
-    def ready(n):
-        for load in loads[1 + 2 * n : 3 + 2 * n]:
-            load.wait()
 
     solve_strip(strip, (low_hi, low_lo), (inv_hi, inv_lo), row_hi, row_lo, factor_ref, ready)
 

time: 190 us -> 190 us (level)
  transfers between devices with their start and end apart: 9 -> 9, of which waited for: 6 -> 6; matrix products, arithmetic and copies ran while one was open for 2% -> 2% of each run, Pallas kernels for 29% -> 28%
where the time goes in v2:
time: 190 us
  Pallas kernels  67.8 us (36%)
  waiting for transfers between devices  56.9 us (30%)
  starting transfers between devices  39.9 us (21%)
  between operations  14.4 us (8%)
  local copies, waits for them, and re-layouts  5.07 us (3%)
  matrix products  3.37 us (2%)
  other arithmetic  1.99 us (1%)
    pallas_call x1, Pallas kernels, cholesky(): pl.pallas_call(cholesky_kernel, in_specs=[pl.BlockSpec(memory_space=pltpu...  38.4 us
    all_to_all x2, waiting for transfers between devices, to_chips(): return lax.all_to_all(x, ('col', 'row'), 0, 0)  28.3 us
    all_to_all x2, starting transfers between devices, to_chips(): return lax.all_to_all(x, ('col', 'row'), 0, 0)  24 us
    all_to_all x1, waiting for transfers between devices, per_device(): lax.all_to_all(jnp.broadcast_to(lead[None], (GR, HALF * 8, BLK)), 'row',...  11.4 us
    all_to_all x1, waiting for transfers between devices, per_device(): lax.all_to_all(jnp.concatenate([for_cols.reshape(NC, 32, BLK), triangle],...  11.2 us
    ppermute x4, starting transfers between devices, swap_cores(): return lax.ppermute(x, 'sub', [(0, 1), (1, 0)])  8.79 us
    pallas_call x1, Pallas kernels, solve_columns(): pl.pallas_call(column_kernel, in_specs=[anywhere] * len(inputs), out_spec...  8.14 us
    pallas_call x1, Pallas kernels, update(): pl.pallas_call(update_kernel, in_specs=[pl.BlockSpec(memory_space=pltpu.S...  6.19 us
  transfers between devices with their start and end apart: 9, of which 6 were waited for; matrix products, arithmetic and copies ran while one was open for 2% of the time, Pallas kernels for 28%

profile of v2, /device:TPU:1, one launch (start us, length us, event | category | flops | bytes accessed | tf_op | source)
XLA Modules:
  0.0 189.5 jit_solution(17490076671446789180)
XLA Ops:
  7.2 3.1 %split_blocks.1 = f32[2048,128]{1,0:T(8,128)} custom-call(f32[2304,128]{1,0:T(8,128)} %bitcast.99, f32[2048,128]{1,0:T(8,128)} %bitcast.93), custom_call_target="tpu_custom_call" | custom-call | bytes 3000000 | tf_op jit(solution)/shard_map/split_blocks/pallas_call | solution.py:520
  10.3 16.5 %all-to-all-start = ((f32[128,16,128]{2,1,0:T(8,128)}), f32[128,16,128]{2,1,0:T(8,128)S(1)}, u32[]{:S(2)}, u32[]{:S(2)}) async-start(f32[128,16,128]{2,1,0:T(8,128)} %bitcast.95), calls=%async_computation | async-start | bytes 2097152 | tf_op jit(solution)/shard_map/all_to_all | solution.py:561
  27.0 28.3 %all-to-all-done = f32[128,16,128]{2,1,0:T(8,128)S(1)} async-done(((f32[128,16,128]{2,1,0:T(8,128)}), f32[128,16,128]{2,1,0:T(8,128)S(1)}, u32[]{:S(2)}, u32[]{:S(2)}) %all-to-all-start) | async-done | bytes 1048608 | tf_op jit(solution)/shard_map/all_to_all | solution.py:561
  56.1 1.9 %fusion.6 = f32[64,8,128]{2,1,0:T(8,128)S(1)} fusion(f32[64,8,128]{2,1,0:T(8,128)S(1)} %bitcast.105, f32[8,8]{0,1:T(8,128)S(1)} %compare_convert_fusion, f32[64,48]{1,0:T(8,128)S(1)} %copy.49, f32[48,48,128]{2,0,1:T(8,128)S(1)} %pad_maximum_fusion), kind=kOutput, calls=%fused_computation.8 | convolution fusion | flops 302252032 | bytes 757760 | tf_op jit(solution)/shard_map/dot_general | solution.py:23
  58.0 3.6 %collective-permute-start = (f32[64,8,128]{2,1,0:T(8,128)S(1)}, f32[64,8,128]{2,1,0:T(8,128)S(1)}, u32[]{:S(2)}, u32[]{:S(2)}) collective-permute-start(f32[64,8,128]{2,1,0:T(8,128)S(1)} %fusion.6), channel_id=1, source_target_pairs={{0,128},{128,0},{1,129},{129,1},{2,130},{130,2},{3,131},{131,3},{4... | collective-permute-start | bytes 786440 | tf_op jit(solution)/shard_map/ppermute | solution.py:569
  61.6 1.2 collective-permute-done
  64.0 3.4 %all-to-all-start.1 = ((f32[8,50,128]{2,1,0:T(8,128)}), f32[8,50,128]{2,1,0:T(8,128)S(1)}, u32[]{:S(2)}, u32[]{:S(2)}) async-start(f32[8,50,128]{2,1,0:T(8,128)} %pad_maximum_fusion.1), calls=%async_computation.1 | async-start | bytes 458752 | tf_op jit(solution)/shard_map/all_to_all | solution.py:612
  67.7 11.2 %all-to-all-done.1 = f32[8,50,128]{2,1,0:T(8,128)S(1)} async-done(((f32[8,50,128]{2,1,0:T(8,128)}), f32[8,50,128]{2,1,0:T(8,128)S(1)}, u32[]{:S(2)}, u32[]{:S(2)}) %all-to-all-start.1) | async-done | bytes 204832 | tf_op jit(solution)/shard_map/all_to_all | solution.py:612
  79.6 1.1 broadcast_in_dim.63
  80.7 3.7 %all-to-all-start.2 = ((f32[16,144,128]{2,1,0:T(8,128)}), f32[16,144,128]{2,1,0:T(8,128)S(1)}, u32[]{:S(2)}, u32[]{:S(2)}) async-start(f32[16,144,128]{2,1,0:T(8,128)} %broadcast_in_dim.63), calls=%async_computation.2 | async-start | bytes 2359296 | tf_op jit(solution)/shard_map/all_to_all | solution.py:618
  84.5 1.5 convolution_bitcast_fusion
  86.9 1.8 collective-permute-done.1.other_ref
  88.6 2.8 %pack.1 = f32[4096,128]{1,0:T(8,128)} custom-call(s32[2,64]{1,0:T(2,128)S(1)} %select_reduce_fusion.inverse_map_ref, f32[48,32,128]{2,1,0:T(8,128)S(1)} %get-tuple-element.45.own_ref, f32[48,32,128]{2,1,0:T(8,128)S(1)} %collective-permute-done.1.other_ref, f32[2,16,8,128]{3,2,1,0:T(8,128)S(1)} %dynamic-slice_bitcast_fusion.panel_ref), custom_call_target="tpu_custom_call" | custom-call | bytes 8000000 | tf_op jit(solution)/shard_map/pack/pallas_call | solution.py:549
  91.4 11.4 %all-to-all-done.2.own_ref = f32[16,144,128]{2,1,0:T(8,128)S(1)} async-done(((f32[16,144,128]{2,1,0:T(8,128)}), f32[16,144,128]{2,1,0:T(8,128)S(1)}, u32[]{:S(2)}, u32[]{:S(2)}) %all-to-all-start.2) | async-done | bytes 1179680 | tf_op jit(solution)/shard_map/all_to_all | solution.py:618
  102.8 2.1 %collective-permute-start.2 = (f32[16,144,128]{2,1,0:T(8,128)S(1)}, f32[16,144,128]{2,1,0:T(8,128)S(1)}, u32[]{:S(2)}, u32[]{:S(2)}) collective-permute-start(f32[16,144,128]{2,1,0:T(8,128)S(1)} %all-to-all-done.2.own_ref), channel_id=1, source_target_pairs={{0,128},{128,0},{1,129},{129,1},{2,130},{130,2},{3,131},{131,3},{4... | collective-permute-start | bytes 3538952 | tf_op jit(solution)/shard_map/ppermute | solution.py:569
  105.6 7.5 %all-to-all-start.3 = ((f32[128,32,128]{2,1,0:T(8,128)}), f32[128,32,128]{2,1,0:T(8,128)}, u32[]{:S(2)}, u32[]{:S(2)}) async-start(f32[128,32,128]{2,1,0:T(8,128)} %bitcast.36), calls=%async_computation.3 | async-start | bytes 4194304 | tf_op jit(solution)/shard_map/all_to_all | solution.py:561
  113.1 1.1 copy-done.1
  114.2 38.4 %cholesky.1 = (bf16[768,768]{1,0:T(8,128)(2,1)}, bf16[768,768]{1,0:T(8,128)(2,1)}, bf16[4,256,256]{2,1,0:T(8,128)(2,1)}, bf16[4,256,256]{2,1,0:T(8,128)(2,1)}, f32[128,1024]{1,0:T(8,128)}) custom-call(s32[3]{0:T(128)} %pad_add_fusion.1.where_ref, f32[16,144,128]{2,1,0:T(8,128)} %copy-done, f32[16,144,128]{2,1,0:T(8,128)} %copy-done.1), custom_call_target="tpu_custom_call" | custom-call | flops 1 | bytes 1 | tf_op jit(solution)/shard_map/cholesky/pallas_call | solution.py:233
  152.6 3.0 %all-gather.3.cloned.1.call-done = f32[128,32,128]{2,1,0:T(8,128)} async-done(((f32[8,32,128]{2,1,0:T(8,128)}), f32[128,32,128]{2,1,0:T(8,128)}) %all-gather.3.cloned.1.call-update) | async-done | bytes 2097168 | tf_op jit(solution)/shard_map/all_gather | solution.py:642
  155.7 8.1 %solve_columns.1 = (bf16[512,1024]{1,0:T(8,128)(2,1)}, bf16[512,1024]{1,0:T(8,128)(2,1)}) custom-call(f32[16,8,32,128]{3,2,1,0:T(8,128)} %bitcast.116, bf16[768,768]{1,0:T(8,128)(2,1)} %get-tuple-element.23.low_hi_hbm, bf16[768,768]{1,0:T(8,128)(2,1)} %get-tuple-element.24.low_lo_hbm, bf16[4,256,256]{2,1,0:T(8,128)(2,1)} %get-tuple-element.25.inv_hi_hbm, ...), custom_call_target="tpu_custom_call" | custom-call | flops 199999995904 | bytes 9000000 | tf_op jit(solution)/shard_map/solve_columns/pallas_call | solution.py:318
  163.8 5.5 %solve_rows.1.own_hbm = f32[256,1024]{1,0:T(8,128)} custom-call(f32[128,32,128]{2,1,0:T(8,128)} %all-to-all-done.3.own_hbm.sums_hbm, bf16[768,768]{1,0:T(8,128)(2,1)} %get-tuple-element.23.low_hi_hbm, bf16[768,768]{1,0:T(8,128)(2,1)} %get-tuple-element.24.low_lo_hbm, bf16[4,256,256]{2,1,0:T(8,128)(2,1)} %get-tuple-element.25.inv_hi_hbm, ...), custom_call_target="tpu_custom_call" | custom-call | flops 2000000000 | bytes 5000000 | tf_op jit(solution)/shard_map/solve_rows/pallas_call | solution.py:364
  169.3 2.4 %collective-permute-start.3 = (f32[256,1024]{1,0:T(8,128)}, f32[256,1024]{1,0:T(8,128)S(1)}, u32[]{:S(2)}, u32[]{:S(2)}) collective-permute-start(f32[256,1024]{1,0:T(8,128)} %solve_rows.1.own_hbm), channel_id=1, source_target_pairs={{0,128},{128,0},{1,129},{129,1},{2,130},{130,2},{3,131},{131,3},{4... | collective-permute-start | bytes 3145736 | tf_op jit(solution)/shard_map/ppermute | solution.py:569
  171.7 3.7 %assemble.1.front_hbm = f32[512,512]{1,0:T(8,128)} custom-call(s32[3]{0:T(128)} %pad_add_fusion.1.where_ref, f32[128,32,128]{2,1,0:T(8,128)} %all-to-all-done.3.own_hbm.sums_hbm, f32[2048,128]{1,0:T(8,128)} %bitcast.94), custom_call_target="tpu_custom_call" | custom-call | flops 1000000000 | bytes 4000000 | tf_op jit(solution)/shard_map/assemble/pallas_call | solution.py:402
  176.5 6.2 %update.1 = (f32[512,1024]{1,0:T(8,128)}, f32[2048,128]{1,0:T(8,128)}) custom-call(s32[3]{0:T(128)} %pad_add_fusion.1.where_ref, f32[256,1024]{1,0:T(8,128)} %solve_rows.1.own_hbm, f32[256,1024]{1,0:T(8,128)} %copy-done.3, bf16[512,1024]{1,0:T(8,128)(2,1)} %get-tuple-element.27.col_hi_hbm, bf16[512,1024]{1,0:T(8,128)(2,1)} %get-tuple-element.29.col_lo_hbm, ...), custom_call_target="tpu_custom_call" | custom-call | flops 2000000000 | bytes 9000000 | tf_op jit(solution)/shard_map/update/pallas_call | solution.py:496
  (63 shorter events, 5.6 us)
Async XLA Ops:
  10.3 16.5 %copy-start.2 = (s32[2,48]{1,0:T(2,128)S(1)}, s32[2,48]{1,0:T(2,128)}, u32[]{:S(2)}) copy-start(s32[2,48]{1,0:T(2,128)} %param.5) | copy-start | bytes 1156
  10.3 45.1 %all-to-all-start = ((f32[128,16,128]{2,1,0:T(8,128)}), f32[128,16,128]{2,1,0:T(8,128)S(1)}, u32[]{:S(2)}, u32[]{:S(2)}) async-start(f32[128,16,128]{2,1,0:T(8,128)} %bitcast.95), calls=%async_computation | async-start | bytes 2097152 | tf_op jit(solution)/shard_map/all_to_all | solution.py:561
  58.0 4.8 %collective-permute-start = (f32[64,8,128]{2,1,0:T(8,128)S(1)}, f32[64,8,128]{2,1,0:T(8,128)S(1)}, u32[]{:S(2)}, u32[]{:S(2)}) collective-permute-start(f32[64,8,128]{2,1,0:T(8,128)S(1)} %fusion.6), channel_id=1, source_target_pairs={{0,128},{128,0},{1,129},{129,1},{2,130},{130,2},{3,131},{131,3},{4... | collective-permute-start | bytes 786440 | tf_op jit(solution)/shard_map/ppermute | solution.py:569
  64.0 14.9 %all-to-all-start.1 = ((f32[8,50,128]{2,1,0:T(8,128)}), f32[8,50,128]{2,1,0:T(8,128)S(1)}, u32[]{:S(2)}, u32[]{:S(2)}) async-start(f32[8,50,128]{2,1,0:T(8,128)} %pad_maximum_fusion.1), calls=%async_computation.1 | async-start | bytes 458752 | tf_op jit(solution)/shard_map/all_to_all | solution.py:612
  80.7 22.1 %all-to-all-start.2 = ((f32[16,144,128]{2,1,0:T(8,128)}), f32[16,144,128]{2,1,0:T(8,128)S(1)}, u32[]{:S(2)}, u32[]{:S(2)}) async-start(f32[16,144,128]{2,1,0:T(8,128)} %broadcast_in_dim.63), calls=%async_computation.2 | async-start | bytes 2359296 | tf_op jit(solution)/shard_map/all_to_all | solution.py:618
  84.4 71.2 %all-gather.3.cloned.1.call-start = ((), (), s32[]{:S(2)}) async-start(), calls=%async_computation.4 | async-start | bytes 2228224 | tf_op jit(solution)/shard_map/all_gather | solution.py:642
  86.1 2.6 %collective-permute-start.1 = (f32[48,32,128]{2,1,0:T(8,128)S(1)}, f32[48,32,128]{2,1,0:T(8,128)S(1)}, u32[]{:S(2)}, u32[]{:S(2)}) collective-permute-start(f32[48,32,128]{2,1,0:T(8,128)S(1)} %get-tuple-element.44), channel_id=1, source_target_pairs={{0,128},{128,0},{1,129},{129,1},{2,130},{130,2},{3,131},{131,3},{4... | collective-permute-start | bytes 2359304 | tf_op jit(solution)/shard_map/ppermute | solution.py:569
  102.8 2.8 %copy-start = (f32[16,144,128]{2,1,0:T(8,128)}, f32[16,144,128]{2,1,0:T(8,128)S(1)}, u32[]{:S(2)}) copy-start(f32[16,144,128]{2,1,0:T(8,128)S(1)} %all-to-all-done.2.own_ref) | copy-start | bytes 3538948
  102.8 10.3 %collective-permute-start.2 = (f32[16,144,128]{2,1,0:T(8,128)S(1)}, f32[16,144,128]{2,1,0:T(8,128)S(1)}, u32[]{:S(2)}, u32[]{:S(2)}) collective-permute-start(f32[16,144,128]{2,1,0:T(8,128)S(1)} %all-to-all-done.2.own_ref), channel_id=1, source_target_pairs={{0,128},{128,0},{1,129},{129,1},{2,130},{130,2},{3,131},{131,3},{4... | collective-permute-start | bytes 3538952 | tf_op jit(solution)/shard_map/ppermute | solution.py:569
  105.6 58.2 %all-to-all-start.3 = ((f32[128,32,128]{2,1,0:T(8,128)}), f32[128,32,128]{2,1,0:T(8,128)}, u32[]{:S(2)}, u32[]{:S(2)}) async-start(f32[128,32,128]{2,1,0:T(8,128)} %bitcast.36), calls=%async_computation.3 | async-start | bytes 4194304 | tf_op jit(solution)/shard_map/all_to_all | solution.py:561
  113.1 1.1 copy-start.1
  169.3 6.1 %collective-permute-start.3 = (f32[256,1024]{1,0:T(8,128)}, f32[256,1024]{1,0:T(8,128)S(1)}, u32[]{:S(2)}, u32[]{:S(2)}) collective-permute-start(f32[256,1024]{1,0:T(8,128)} %solve_rows.1.own_hbm), channel_id=1, source_target_pairs={{0,128},{128,0},{1,129},{129,1},{2,130},{130,2},{3,131},{131,3},{4... | collective-permute-start | bytes 3145736 | tf_op jit(solution)/shard_map/ppermute | solution.py:569
  175.5 1.0 copy-start.3
Sparse Core Ops, SparseCore 0:
  102.9 52.6 all-gather.2

commit v3 on v2

--- a/solution.py
+++ b/solution.py
@@ -379,11 +379,19 @@
     )(rows_in, *factor_parts)
 
 
-def front_kernel(where_ref, sums_hbm, entry_ref, front_ref, sums_ref, sem):
+def front_kernel(
+    where_ref, sums_hbm, entry_hbm, front_hbm, sums_ref, entry_ref, front_ref, sems
+):
     grid_row, grid_col = where_ref[1], where_ref[2]
-    load = pltpu.make_async_copy(sums_hbm.at[:, :16, :], sums_ref, sem)
-    load.start()
-    load.wait()
+    loads = [
+        pltpu.make_async_copy(sums_hbm.at[:, :16, :], sums_ref, sems.at[0]),
+        pltpu.make_async_copy(entry_hbm, entry_ref, sems.at[1]),
+    ]
+    for load in loads:
+        load.start()
+    for load in loads:
+        load.wait()
+    stores = []
     for b in range(4):
         if b % 2 == 0:
             blocks = jnp.swapaxes(sums_ref[:, b * 4 : b * 4 + 8, :], 0, 1)
@@ -395,20 +403,30 @@
                 sums = jnp.where(grid_row >= grid_col, sums, sums.T)
             entry = entry_ref[pl.ds(b * STRIP + d, BLK, stride=4), :]
             front_ref[b * BLK : (b + 1) * BLK, d * BLK : (d + 1) * BLK] = entry + sums
+        rows = slice(b * BLK, (b + 1) * BLK)
+        stores.append(pltpu.make_async_copy(front_ref.at[rows], front_hbm.at[rows], sems.at[2 + b]))
+        stores[-1].start()
+    for store in stores:
+        store.wait()
 
 
 def assemble(where, rows_in, entries):
-    whole = pl.BlockSpec(memory_space=pltpu.VMEM)
+    anywhere = pl.BlockSpec(memory_space=pl.ANY)
     return pl.pallas_call(
         front_kernel,
         in_specs=[
             pl.BlockSpec(memory_space=pltpu.SMEM),
-            pl.BlockSpec(memory_space=pl.ANY),
-            whole,
+            anywhere,
+            anywhere,
         ],
-        out_specs=whole,
+        out_specs=anywhere,
         out_shape=jax.ShapeDtypeStruct((STRIP, STRIP), F32),
-        scratch_shapes=[pltpu.VMEM((BLK, 16, BLK), F32), pltpu.SemaphoreType.DMA(())],
+        scratch_shapes=[
+            pltpu.VMEM((BLK, 16, BLK), F32),
+            pltpu.VMEM((4 * STRIP, BLK), F32),
+            pltpu.VMEM((STRIP, STRIP), F32),
+            pltpu.SemaphoreType.DMA((6,)),
+        ],
         compiler_params=pltpu.CompilerParams(vmem_limit_bytes=60 * 2**20),
         cost_estimate=pl.CostEstimate(
             flops=1_000_000_000, bytes_accessed=4_000_000, transcendentals=0
@@ -470,6 +488,7 @@
 
     factor_store = pltpu.make_async_copy(factor_ref, factor_hbm, sems.at[6])
     factor_store.start()
+    stores = [factor_store]
     product[...] = dot_split(split(factor_ref[...]), (col_hi[...], col_lo[...]))
     for b in range(4):
         for d in range(4):
@@ -480,10 +499,11 @@
             if d == 0:
                 trail = jnp.where(grid_col >= NPB, trail, 0.0)
             out_ref[pl.ds(b * STRIP + d, BLK, stride=4), :] = front_ref[rows, cols] - trail
-    out_store = pltpu.make_async_copy(out_ref, out_hbm, sems.at[7])
-    out_store.start()
-    factor_store.wait()
-    out_store.wait()
+        spot = slice(b * STRIP, (b + 1) * STRIP)
+        stores.append(pltpu.make_async_copy(out_ref.at[spot], out_hbm.at[spot], sems.at[7 + b]))
+        stores[-1].start()
+    for store in stores:
+        store.wait()
 
 
 def update(where, own, other, columns, front, top):
@@ -499,7 +519,7 @@
         out_specs=[anywhere] * 2,
         out_shape=outputs,
         scratch_shapes=[pltpu.VMEM(x.shape, x.dtype) for x in (*inputs[2:], *outputs)]
-        + [pltpu.VMEM((STRIP, STRIP), F32), pltpu.SemaphoreType.DMA((8,))],
+        + [pltpu.VMEM((STRIP, STRIP), F32), pltpu.SemaphoreType.DMA((11,))],
         compiler_params=pltpu.CompilerParams(vmem_limit_bytes=60 * 2**20),
         cost_estimate=pl.CostEstimate(
             flops=2_000_000_000, bytes_accessed=9_000_000, transcendentals=0

time: 190 us -> 190 us (level)
  no operation moved by 1% of the time
where the time goes in v3:
time: 190 us; the launch traced here: 189 us
  Pallas kernels  67.4 us (35%)
  waiting for transfers between devices  56.9 us (30%)
  starting transfers between devices  39.9 us (21%)
  between operations  14.4 us (8%)
  local copies, waits for them, and re-layouts  5.07 us (3%)
  matrix products  3.37 us (2%)
  other arithmetic  1.99 us (1%)
    pallas_call x1, Pallas kernels, cholesky(): pl.pallas_call(cholesky_kernel, in_specs=[pl.BlockSpec(memory_space=pltpu...  38.4 us
    all_to_all x2, waiting for transfers between devices, to_chips(): return lax.all_to_all(x, ('col', 'row'), 0, 0)  28.3 us
    all_to_all x2, starting transfers between devices, to_chips(): return lax.all_to_all(x, ('col', 'row'), 0, 0)  24 us
    all_to_all x1, waiting for transfers between devices, per_device(): lax.all_to_all(jnp.broadcast_to(lead[None], (GR, HALF * 8, BLK)), 'row',...  11.4 us
    all_to_all x1, waiting for transfers between devices, per_device(): lax.all_to_all(jnp.concatenate([for_cols.reshape(NC, 32, BLK), triangle],...  11.2 us
    ppermute x4, starting transfers between devices, swap_cores(): return lax.ppermute(x, 'sub', [(0, 1), (1, 0)])  8.79 us
    pallas_call x1, Pallas kernels, solve_columns(): pl.pallas_call(column_kernel, in_specs=[anywhere] * len(inputs), out_spec...  8.14 us
    pallas_call x1, Pallas kernels, update(): pl.pallas_call(update_kernel, in_specs=[pl.BlockSpec(memory_space=pltpu.S...  6.1 us
  transfers between devices with their start and end apart: 9, of which 6 were waited for; matrix products, arithmetic and copies ran while one was open for 2% of the time, Pallas kernels for 28%

profile of v3, /device:TPU:1, one launch (start us, length us, event | category | flops | bytes accessed | tf_op | source)
XLA Modules:
  0.0 189.1 jit_solution(773954027933324776)
XLA Ops:
  7.2 3.1 %split_blocks.1 = f32[2048,128]{1,0:T(8,128)} custom-call(f32[2304,128]{1,0:T(8,128)} %bitcast.99, f32[2048,128]{1,0:T(8,128)} %bitcast.93), custom_call_target="tpu_custom_call" | custom-call | bytes 3000000 | tf_op jit(solution)/shard_map/split_blocks/pallas_call | solution.py:540
  10.3 16.5 %all-to-all-start = ((f32[128,16,128]{2,1,0:T(8,128)}), f32[128,16,128]{2,1,0:T(8,128)S(1)}, u32[]{:S(2)}, u32[]{:S(2)}) async-start(f32[128,16,128]{2,1,0:T(8,128)} %bitcast.95), calls=%async_computation | async-start | bytes 2097152 | tf_op jit(solution)/shard_map/all_to_all | solution.py:581
  27.0 28.3 %all-to-all-done = f32[128,16,128]{2,1,0:T(8,128)S(1)} async-done(((f32[128,16,128]{2,1,0:T(8,128)}), f32[128,16,128]{2,1,0:T(8,128)S(1)}, u32[]{:S(2)}, u32[]{:S(2)}) %all-to-all-start) | async-done | bytes 1048608 | tf_op jit(solution)/shard_map/all_to_all | solution.py:581
  56.1 1.9 %fusion.6 = f32[64,8,128]{2,1,0:T(8,128)S(1)} fusion(f32[64,8,128]{2,1,0:T(8,128)S(1)} %bitcast.105, f32[8,8]{0,1:T(8,128)S(1)} %compare_convert_fusion, f32[64,48]{1,0:T(8,128)S(1)} %copy.49, f32[48,48,128]{2,0,1:T(8,128)S(1)} %pad_maximum_fusion), kind=kOutput, calls=%fused_computation.8 | convolution fusion | flops 302252032 | bytes 757760 | tf_op jit(solution)/shard_map/dot_general | solution.py:23
  58.0 3.6 %collective-permute-start = (f32[64,8,128]{2,1,0:T(8,128)S(1)}, f32[64,8,128]{2,1,0:T(8,128)S(1)}, u32[]{:S(2)}, u32[]{:S(2)}) collective-permute-start(f32[64,8,128]{2,1,0:T(8,128)S(1)} %fusion.6), channel_id=1, source_target_pairs={{0,128},{128,0},{1,129},{129,1},{2,130},{130,2},{3,131},{131,3},{4... | collective-permute-start | bytes 786440 | tf_op jit(solution)/shard_map/ppermute | solution.py:589
  61.6 1.2 collective-permute-done
  64.0 3.4 %all-to-all-start.1 = ((f32[8,50,128]{2,1,0:T(8,128)}), f32[8,50,128]{2,1,0:T(8,128)S(1)}, u32[]{:S(2)}, u32[]{:S(2)}) async-start(f32[8,50,128]{2,1,0:T(8,128)} %pad_maximum_fusion.1), calls=%async_computation.1 | async-start | bytes 458752 | tf_op jit(solution)/shard_map/all_to_all | solution.py:632
  67.7 11.2 %all-to-all-done.1 = f32[8,50,128]{2,1,0:T(8,128)S(1)} async-done(((f32[8,50,128]{2,1,0:T(8,128)}), f32[8,50,128]{2,1,0:T(8,128)S(1)}, u32[]{:S(2)}, u32[]{:S(2)}) %all-to-all-start.1) | async-done | bytes 204832 | tf_op jit(solution)/shard_map/all_to_all | solution.py:632
  79.6 1.1 broadcast_in_dim.63
  80.7 3.7 %all-to-all-start.2 = ((f32[16,144,128]{2,1,0:T(8,128)}), f32[16,144,128]{2,1,0:T(8,128)S(1)}, u32[]{:S(2)}, u32[]{:S(2)}) async-start(f32[16,144,128]{2,1,0:T(8,128)} %broadcast_in_dim.63), calls=%async_computation.2 | async-start | bytes 2359296 | tf_op jit(solution)/shard_map/all_to_all | solution.py:638
  84.5 1.5 convolution_bitcast_fusion
  86.9 1.8 collective-permute-done.1.other_ref
  88.6 2.8 %pack.1 = f32[4096,128]{1,0:T(8,128)} custom-call(s32[2,64]{1,0:T(2,128)S(1)} %select_reduce_fusion.inverse_map_ref, f32[48,32,128]{2,1,0:T(8,128)S(1)} %get-tuple-element.45.own_ref, f32[48,32,128]{2,1,0:T(8,128)S(1)} %collective-permute-done.1.other_ref, f32[2,16,8,128]{3,2,1,0:T(8,128)S(1)} %dynamic-slice_bitcast_fusion.panel_ref), custom_call_target="tpu_custom_call" | custom-call | bytes 8000000 | tf_op jit(solution)/shard_map/pack/pallas_call | solution.py:569
  91.4 11.4 %all-to-all-done.2.own_ref = f32[16,144,128]{2,1,0:T(8,128)S(1)} async-done(((f32[16,144,128]{2,1,0:T(8,128)}), f32[16,144,128]{2,1,0:T(8,128)S(1)}, u32[]{:S(2)}, u32[]{:S(2)}) %all-to-all-start.2) | async-done | bytes 1179680 | tf_op jit(solution)/shard_map/all_to_all | solution.py:638
  102.8 2.1 %collective-permute-start.2 = (f32[16,144,128]{2,1,0:T(8,128)S(1)}, f32[16,144,128]{2,1,0:T(8,128)S(1)}, u32[]{:S(2)}, u32[]{:S(2)}) collective-permute-start(f32[16,144,128]{2,1,0:T(8,128)S(1)} %all-to-all-done.2.own_ref), channel_id=1, source_target_pairs={{0,128},{128,0},{1,129},{129,1},{2,130},{130,2},{3,131},{131,3},{4... | collective-permute-start | bytes 3538952 | tf_op jit(solution)/shard_map/ppermute | solution.py:589
  105.6 7.5 %all-to-all-start.3 = ((f32[128,32,128]{2,1,0:T(8,128)}), f32[128,32,128]{2,1,0:T(8,128)}, u32[]{:S(2)}, u32[]{:S(2)}) async-start(f32[128,32,128]{2,1,0:T(8,128)} %bitcast.36), calls=%async_computation.3 | async-start | bytes 4194304 | tf_op jit(solution)/shard_map/all_to_all | solution.py:581
  113.1 1.1 copy-done.1
  114.2 38.4 %cholesky.1 = (bf16[768,768]{1,0:T(8,128)(2,1)}, bf16[768,768]{1,0:T(8,128)(2,1)}, bf16[4,256,256]{2,1,0:T(8,128)(2,1)}, bf16[4,256,256]{2,1,0:T(8,128)(2,1)}, f32[128,1024]{1,0:T(8,128)}) custom-call(s32[3]{0:T(128)} %pad_add_fusion.1.where_ref, f32[16,144,128]{2,1,0:T(8,128)} %copy-done, f32[16,144,128]{2,1,0:T(8,128)} %copy-done.1), custom_call_target="tpu_custom_call" | custom-call | flops 1 | bytes 1 | tf_op jit(solution)/shard_map/cholesky/pallas_call | solution.py:233
  152.6 3.0 %all-gather.3.cloned.1.call-done = f32[128,32,128]{2,1,0:T(8,128)} async-done(((f32[8,32,128]{2,1,0:T(8,128)}), f32[128,32,128]{2,1,0:T(8,128)}) %all-gather.3.cloned.1.call-update) | async-done | bytes 2097168 | tf_op jit(solution)/shard_map/all_gather | solution.py:662
  155.7 8.1 %solve_columns.1 = (bf16[512,1024]{1,0:T(8,128)(2,1)}, bf16[512,1024]{1,0:T(8,128)(2,1)}) custom-call(f32[16,8,32,128]{3,2,1,0:T(8,128)} %bitcast.116, bf16[768,768]{1,0:T(8,128)(2,1)} %get-tuple-element.23.low_hi_hbm, bf16[768,768]{1,0:T(8,128)(2,1)} %get-tuple-element.24.low_lo_hbm, bf16[4,256,256]{2,1,0:T(8,128)(2,1)} %get-tuple-element.25.inv_hi_hbm, ...), custom_call_target="tpu_custom_call" | custom-call | flops 199999995904 | bytes 9000000 | tf_op jit(solution)/shard_map/solve_columns/pallas_call | solution.py:318
  163.8 5.5 %solve_rows.1.own_hbm = f32[256,1024]{1,0:T(8,128)} custom-call(f32[128,32,128]{2,1,0:T(8,128)} %all-to-all-done.3.own_hbm.sums_hbm, bf16[768,768]{1,0:T(8,128)(2,1)} %get-tuple-element.23.low_hi_hbm, bf16[768,768]{1,0:T(8,128)(2,1)} %get-tuple-element.24.low_lo_hbm, bf16[4,256,256]{2,1,0:T(8,128)(2,1)} %get-tuple-element.25.inv_hi_hbm, ...), custom_call_target="tpu_custom_call" | custom-call | flops 2000000000 | bytes 5000000 | tf_op jit(solution)/shard_map/solve_rows/pallas_call | solution.py:364
  169.3 2.4 %collective-permute-start.3 = (f32[256,1024]{1,0:T(8,128)}, f32[256,1024]{1,0:T(8,128)S(1)}, u32[]{:S(2)}, u32[]{:S(2)}) collective-permute-start(f32[256,1024]{1,0:T(8,128)} %solve_rows.1.own_hbm), channel_id=1, source_target_pairs={{0,128},{128,0},{1,129},{129,1},{2,130},{130,2},{3,131},{131,3},{4... | collective-permute-start | bytes 3145736 | tf_op jit(solution)/shard_map/ppermute | solution.py:589
  171.7 3.4 %assemble.1.front_hbm = f32[512,512]{1,0:T(8,128)} custom-call(s32[3]{0:T(128)} %pad_add_fusion.1.where_ref, f32[128,32,128]{2,1,0:T(8,128)} %all-to-all-done.3.own_hbm.sums_hbm, f32[2048,128]{1,0:T(8,128)} %bitcast.94), custom_call_target="tpu_custom_call" | custom-call | flops 1000000000 | bytes 4000000 | tf_op jit(solution)/shard_map/assemble/pallas_call | solution.py:415
  176.1 6.1 %update.1 = (f32[512,1024]{1,0:T(8,128)}, f32[2048,128]{1,0:T(8,128)}) custom-call(s32[3]{0:T(128)} %pad_add_fusion.1.where_ref, f32[256,1024]{1,0:T(8,128)} %solve_rows.1.own_hbm, f32[256,1024]{1,0:T(8,128)} %copy-done.3, bf16[512,1024]{1,0:T(8,128)(2,1)} %get-tuple-element.27.col_hi_hbm, bf16[512,1024]{1,0:T(8,128)(2,1)} %get-tuple-element.29.col_lo_hbm, ...), custom_call_target="tpu_custom_call" | custom-call | flops 2000000000 | bytes 9000000 | tf_op jit(solution)/shard_map/update/pallas_call | solution.py:516
  (63 shorter events, 5.6 us)
Async XLA Ops:
  10.3 16.5 %copy-start.2 = (s32[2,48]{1,0:T(2,128)S(1)}, s32[2,48]{1,0:T(2,128)}, u32[]{:S(2)}) copy-start(s32[2,48]{1,0:T(2,128)} %param.5) | copy-start | bytes 1156
  10.3 45.1 %all-to-all-start = ((f32[128,16,128]{2,1,0:T(8,128)}), f32[128,16,128]{2,1,0:T(8,128)S(1)}, u32[]{:S(2)}, u32[]{:S(2)}) async-start(f32[128,16,128]{2,1,0:T(8,128)} %bitcast.95), calls=%async_computation | async-start | bytes 2097152 | tf_op jit(solution)/shard_map/all_to_all | solution.py:581
  58.0 4.8 %collective-permute-start = (f32[64,8,128]{2,1,0:T(8,128)S(1)}, f32[64,8,128]{2,1,0:T(8,128)S(1)}, u32[]{:S(2)}, u32[]{:S(2)}) collective-permute-start(f32[64,8,128]{2,1,0:T(8,128)S(1)} %fusion.6), channel_id=1, source_target_pairs={{0,128},{128,0},{1,129},{129,1},{2,130},{130,2},{3,131},{131,3},{4... | collective-permute-start | bytes 786440 | tf_op jit(solution)/shard_map/ppermute | solution.py:589
  64.0 14.9 %all-to-all-start.1 = ((f32[8,50,128]{2,1,0:T(8,128)}), f32[8,50,128]{2,1,0:T(8,128)S(1)}, u32[]{:S(2)}, u32[]{:S(2)}) async-start(f32[8,50,128]{2,1,0:T(8,128)} %pad_maximum_fusion.1), calls=%async_computation.1 | async-start | bytes 458752 | tf_op jit(solution)/shard_map/all_to_all | solution.py:632
  80.7 22.1 %all-to-all-start.2 = ((f32[16,144,128]{2,1,0:T(8,128)}), f32[16,144,128]{2,1,0:T(8,128)S(1)}, u32[]{:S(2)}, u32[]{:S(2)}) async-start(f32[16,144,128]{2,1,0:T(8,128)} %broadcast_in_dim.63), calls=%async_computation.2 | async-start | bytes 2359296 | tf_op jit(solution)/shard_map/all_to_all | solution.py:638
  84.4 71.2 %all-gather.3.cloned.1.call-start = ((), (), s32[]{:S(2)}) async-start(), calls=%async_computation.4 | async-start | bytes 2228224 | tf_op jit(solution)/shard_map/all_gather | solution.py:662
  86.1 2.6 %collective-permute-start.1 = (f32[48,32,128]{2,1,0:T(8,128)S(1)}, f32[48,32,128]{2,1,0:T(8,128)S(1)}, u32[]{:S(2)}, u32[]{:S(2)}) collective-permute-start(f32[48,32,128]{2,1,0:T(8,128)S(1)} %get-tuple-element.44), channel_id=1, source_target_pairs={{0,128},{128,0},{1,129},{129,1},{2,130},{130,2},{3,131},{131,3},{4... | collective-permute-start | bytes 2359304 | tf_op jit(solution)/shard_map/ppermute | solution.py:589
  102.8 2.8 %copy-start = (f32[16,144,128]{2,1,0:T(8,128)}, f32[16,144,128]{2,1,0:T(8,128)S(1)}, u32[]{:S(2)}) copy-start(f32[16,144,128]{2,1,0:T(8,128)S(1)} %all-to-all-done.2.own_ref) | copy-start | bytes 3538948
  102.8 10.3 %collective-permute-start.2 = (f32[16,144,128]{2,1,0:T(8,128)S(1)}, f32[16,144,128]{2,1,0:T(8,128)S(1)}, u32[]{:S(2)}, u32[]{:S(2)}) collective-permute-start(f32[16,144,128]{2,1,0:T(8,128)S(1)} %all-to-all-done.2.own_ref), channel_id=1, source_target_pairs={{0,128},{128,0},{1,129},{129,1},{2,130},{130,2},{3,131},{131,3},{4... | collective-permute-start | bytes 3538952 | tf_op jit(solution)/shard_map/ppermute | solution.py:589
  105.6 58.2 %all-to-all-start.3 = ((f32[128,32,128]{2,1,0:T(8,128)}), f32[128,32,128]{2,1,0:T(8,128)}, u32[]{:S(2)}, u32[]{:S(2)}) async-start(f32[128,32,128]{2,1,0:T(8,128)} %bitcast.36), calls=%async_computation.3 | async-start | bytes 4194304 | tf_op jit(solution)/shard_map/all_to_all | solution.py:581
  113.1 1.1 copy-start.1
  169.3 5.8 %collective-permute-start.3 = (f32[256,1024]{1,0:T(8,128)}, f32[256,1024]{1,0:T(8,128)S(1)}, u32[]{:S(2)}, u32[]{:S(2)}) collective-permute-start(f32[256,1024]{1,0:T(8,128)} %solve_rows.1.own_hbm), channel_id=1, source_target_pairs={{0,128},{128,0},{1,129},{129,1},{2,130},{130,2},{3,131},{131,3},{4... | collective-permute-start | bytes 3145736 | tf_op jit(solution)/shard_map/ppermute | solution.py:589
  175.1 1.0 copy-start.3
Sparse Core Ops, SparseCore 0:
  102.9 52.6 all-gather.2
